TPU v7x, 32 devices: a whole 2x2x4 slice. The times are simulated.
32 devices in a mesh: blk: 8 (over y, x, core), rep: 4 (over z).
Axes of the slice: x: 2, y: 2, z: 4, core: 2. Of those that a mesh axis runs over, the one named last changes fastest.
Arguments:
- coords: float32 [192, 4096], P('rep', 'blk'), may hold values from -4 to 4
- eigvecs: float32 [128, 4096], P(None, ('blk', 'rep')), may hold values from -0.36 to 0.36
- nbr_list: int32 [32, 8], P('blk'), may hold values from 0 to 31, as said below
- nbr_count: int32 [32], P('blk'), may hold values from 2 to 8, as said below
Outputs:
- smoothed: float32 [128, 4096], P(None, ('blk', 'rep'))
Inputs may be any that keep to these rules, and one draw needn't show every extreme that they name: `nbr_count`: the largest count is exactly 8 in every draw; counts differ from block to block. `nbr_list`: the first nbr_count entries of a row are distinct block indices; entries after them are not used.
All inputs are finite; a program needn't handle non-finite values.
Results may differ from a plain program's by a relative error of at most 0.0003.
Values sent between devices are 32-bit elements; how exact they have to be, the bound alone decides.
No kernel may reach another device: no remote copies, remote signals or barrier semaphores. Data moves between devices by JAX's collectives and lax.ppermute only.
A program may use at most 64 MiB of HBM per device.

v0:
```python
import functools

import jax
import jax.numpy as jnp
from jax import lax
from jax.experimental import pallas as pl
from jax.experimental.pallas import tpu as pltpu
from jax.sharding import PartitionSpec as P


TRANSFER_FLOPS = 62 * 10**8


def halves(value):
    high = value.astype(jnp.bfloat16)
    return high, (value - high.astype(jnp.float32)).astype(jnp.bfloat16)


def stacked(value, order, axis):
    high, low = halves(value)
    return jnp.concatenate([{"h": high, "l": low}[letter] for letter in order], axis=axis)


def lists_kernel(list_ref, count_ref, out_ref):
    rank = lax.axis_index("rep")
    for slot in range(out_ref.shape[0]):
        listed = jnp.where(slot < count_ref[rank], list_ref[rank, slot], -1)
        out_ref[slot : slot + 1, :] = jnp.full((1, out_ref.shape[1]), listed.astype(jnp.float32))


def copy_kernel(before_ref, in_ref, out_ref):
    out_ref[...] = in_ref[...]


def group_kernel(piece_count, *refs):
    piece_refs, vec_refs, out_ref = refs[:piece_count], refs[piece_count:-1], refs[-1]
    piece_feats = piece_refs[0].shape[0]
    width = vec_refs[0].shape[1]
    feat_count = piece_count * piece_feats
    rank = lax.axis_index("rep")
    for piece, ref in enumerate(piece_refs):
        out_ref[piece * piece_feats : (piece + 1) * piece_feats, :] = ref[...]
    for spot, ref in enumerate(vec_refs[::-1]):
        span = pl.ds(pl.multiple_of((rank ^ spot) * width, width), width)
        out_ref[feat_count:, span] = ref[...]


def columns_kernel(feat_count, group_ref, col_ref, vec_ref):
    chunk = 2 * vec_ref.shape[0]
    cols = group_ref[:feat_count, :]
    col_ref[...] = stacked(cols.T, "hhl", 1)
    vecs = group_ref[feat_count:, :] * jnp.exp(jnp.sum(cols * cols, axis=0, keepdims=True) * (-1.0 / feat_count))
    for start in range(0, cols.shape[1], chunk):
        vec_ref[:, 3 * start : 3 * (start + chunk)] = stacked(vecs[:, start : start + chunk], "hhl", 1)


def rows_kernel(feat_count, *refs):
    panel_refs, (row_ref, scale_ref, mask_ref) = refs[:-3], refs[-3:]
    width = panel_refs[0].shape[1]
    group_blocks = mask_ref.shape[0] // 2
    blk_index = lax.axis_index("blk")
    for place, ref in enumerate(panel_refs):
        span = slice(place * width, (place + 1) * width)
        rows = ref[:feat_count, :]
        scale_ref[:, span] = jnp.exp(jnp.sum(rows * rows, axis=0, keepdims=True) * (-1.0 / feat_count))
        row_ref[:, span] = stacked(rows * (2.0 / feat_count), "hlh", 0)
        lists = ref[feat_count:, :]
        for spot in range(2 * group_blocks):
            column = (blk_index ^ (spot // group_blocks)) * group_blocks + spot % group_blocks
            hits = jnp.where(lists == column.astype(jnp.float32), 1.0, 0.0)
            mask_ref[spot : spot + 1, span] = jnp.max(hits, axis=0, keepdims=True)


def apply_kernel(row_ref, scale_ref, mask_ref, *refs):
    own_cols, own_vecs, sibling_cols, sibling_vecs, *out_refs = refs
    width = out_refs[0].shape[1]
    group_cols = own_cols.shape[0]
    chunk = 2 * width
    pairs = range(len(out_refs) // 2)
    totals = [None for _ in pairs]
    for group, (col_ref, vec_ref) in enumerate(((own_cols, own_vecs), (sibling_cols, sibling_vecs))):
        for start in range(0, group_cols, chunk):
            at = (group * group_cols + start) // width
            for pair in pairs:
                span = slice(pair * chunk, (pair + 1) * chunk)
                inner = jnp.dot(
                    col_ref[start : start + chunk, :], row_ref[:, span], preferred_element_type=jnp.float32
                )
                both = [jnp.broadcast_to(mask_ref[spot : spot + 1, span], (width, chunk)) for spot in (at, at + 1)]
                weight = stacked(jnp.exp(inner) * jnp.concatenate(both, axis=0), "hlh", 0)
                vecs = vec_ref[:, 3 * start : 3 * (start + chunk)]
                added = jnp.dot(vecs, weight, preferred_element_type=jnp.float32)
                totals[pair] = added if totals[pair] is None else totals[pair] + added
    for pair in pairs:
        total = totals[pair] * scale_ref[:, pair * chunk : (pair + 1) * chunk]
        out_refs[2 * pair][...] = total[:, :width]
        out_refs[2 * pair + 1][...] = total[:, width:]


def swapped(value, axis, step):
    count = lax.axis_size(axis)
    return lax.ppermute(value, axis, [(source, source ^ step) for source in range(count)])


def shards(coords, eigvecs, nbr_list, nbr_count):
    cycle_size = lax.axis_size("blk")
    rep_size = lax.axis_size("rep")
    rep_index = lax.axis_index("rep")
    group_blocks, slot_count = nbr_list.shape
    eig_count, width = eigvecs.shape
    piece_feats, group_cols = coords.shape
    feat_count = rep_size * piece_feats
    f32, bf16 = jnp.float32, jnp.bfloat16
    shape = jax.ShapeDtypeStruct
    smem = pl.BlockSpec(memory_space=pltpu.SMEM)
    vmem = pl.BlockSpec(memory_space=pltpu.VMEM)
    anywhere = pl.BlockSpec(memory_space=pl.ANY)
    params = pltpu.CompilerParams(vmem_limit_bytes=(8 + group_blocks) * 1024 * 1024)
    hint = pl.CostEstimate(flops=TRANSFER_FLOPS, bytes_accessed=1024 * 1024, transcendentals=0)

    send_order = [1, 3, 2, *range(4, rep_size)]
    pieces = {step: swapped(coords, "rep", step) for step in send_order}
    near = pieces[1]
    pieces = [coords] + [pieces[step] for step in send_order]
    late_vecs = pl.pallas_call(
        copy_kernel,
        in_specs=[anywhere, vmem],
        out_shape=shape(eigvecs.shape, f32),
        compiler_params=params,
    )(near, eigvecs)
    vecs = [swapped(late_vecs, "rep", step) for step in range(rep_size - 1, 0, -1)] + [late_vecs]
    lists = pl.pallas_call(
        lists_kernel,
        in_specs=[smem, smem],
        out_shape=shape((slot_count, width), f32),
        compiler_params=params,
    )(nbr_list, nbr_count)

    own_block = [lax.dynamic_slice_in_dim(piece, rep_index * width, width, 1) for piece in pieces]
    panel = jnp.concatenate([*own_block, lists], axis=0)
    steps = list(range(0, cycle_size, 2))
    panels = [panel] + [swapped(panel, "blk", step) for step in steps[1:]]

    own_group = pl.pallas_call(
        functools.partial(group_kernel, rep_size),
        out_shape=shape((feat_count + eig_count, group_cols), f32),
        compiler_params=params,
    )(*pieces, *vecs)
    sibling_group = swapped(own_group, "blk", 1)

    def columns_of(group):
        return pl.pallas_call(
            functools.partial(columns_kernel, feat_count),
            out_shape=[shape((group_cols, 3 * feat_count), bf16), shape((eig_count, 3 * group_cols), bf16)],
            compiler_params=params,
        )(group)

    row_count = len(panels) * width
    rows = pl.pallas_call(
        functools.partial(rows_kernel, feat_count),
        out_shape=[
            shape((3 * feat_count, row_count), bf16),
            shape((1, row_count), f32),
            shape((2 * group_blocks, row_count), f32),
        ],
        compiler_params=params,
        cost_estimate=hint,
    )(*panels)
    columns = [*columns_of(own_group), *columns_of(sibling_group)]
    tiles = pl.pallas_call(
        apply_kernel,
        out_shape=[shape((eig_count, width), f32)] * len(panels),
        compiler_params=params,
    )(*rows, *columns)
    total = tiles[0]
    for place in range(len(steps) - 1, 0, -1):
        total = total + swapped(tiles[place], "blk", steps[place])
    return total


def solution(mesh):
    return jax.shard_map(
        shards,
        mesh=mesh,
        in_specs=(P("rep", "blk"), P(None, ("blk", "rep")), P("blk", None), P("blk")),
        out_specs=P(None, ("blk", "rep")),
        check_vma=False,
    )
```

profile of v0, /device:TPU:0, one launch (start us, length us, event | category | flops | bytes accessed | tf_op | source)
XLA Modules:
  0.0 32.9 jit_solution(9155499274180400565)
XLA Ops:
  0.0 0.0 copy-start.1
  0.0 5.0 %collective-permute-start.1 = (f32[48,512]{1,0:T(8,128)}, f32[48,512]{1,0:T(8,128)S(1)}, u32[]{:S(2)}, u32[]{:S(2)}) collective-permute-start(f32[48,512]{1,0:T(8,128)} %refs_0_.1), channel_id=1, source_target_pairs={{0,3},{1,2},{2,1},{3,0},{4,7},{5,6},{6,5},{7,4},{8,11},{9,10},{10,... | collective-permute-start | bytes 294920 | tf_op jit(solution)/shard_map/ppermute | solution.py:102
  5.1 0.0 collective-permute-start
  5.1 0.6 %collective-permute-start.2 = (f32[48,512]{1,0:T(8,128)}, f32[48,512]{1,0:T(8,128)S(1)}, u32[]{:S(2)}, u32[]{:S(2)}) collective-permute-start(f32[48,512]{1,0:T(8,128)} %refs_0_.1), channel_id=1, source_target_pairs={{0,2},{1,3},{2,0},{3,1},{4,6},{5,7},{6,4},{7,5},{8,10},{9,11},{10,... | collective-permute-start | bytes 294920 | tf_op jit(solution)/shard_map/ppermute | solution.py:102
  5.7 0.0 copy-start.2
  5.7 0.7 %copy-done.2 = s32[4,8]{1,0:T(4,128)S(1)} copy-done((s32[4,8]{1,0:T(4,128)S(1)}, s32[4,8]{1,0:T(4,128)}, u32[]{:S(2)}) %copy-start.2) | copy-done | bytes 152
  6.4 0.0 copy-start.3
  6.4 0.7 %copy-done.3 = s32[4]{0:T(128)S(1)} copy-done((s32[4]{0:T(128)S(1)}, s32[4]{0:T(128)}, u32[]{:S(2)}) %copy-start.3) | copy-done | bytes 40
  7.0 0.6 %shard_map.46 = f32[8,128]{1,0:T(8,128)S(1)} custom-call(s32[4,8]{1,0:T(4,128)S(1)} %copy-done.2, s32[4]{0:T(128)S(1)} %copy-done.3), custom_call_target="tpu_custom_call" | custom-call | tf_op jit(solution)/shard_map/pallas_call | solution.py:132
  7.6 0.7 %dynamic-slice_dynamic-update-slice_fusion.3 = f32[200,128]{1,0:T(8,128)S(1)} fusion(f32[48,512]{1,0:T(8,128)} %refs_0_.1, s32[]{:T(128)S(6)} %select_n.2), kind=kLoop, calls=%fused_computation.4 | loop fusion | bytes 49156
  8.4 2.9 %collective-permute-done.before_ref.refs_1_ = f32[48,512]{1,0:T(8,128)S(1)} collective-permute-done((f32[48,512]{1,0:T(8,128)}, f32[48,512]{1,0:T(8,128)S(1)}, u32[]{:S(2)}, u32[]{:S(2)}) %collective-permute-start) | collective-permute-done | bytes 98336 | tf_op jit(solution)/shard_map/ppermute | solution.py:102
  11.3 0.0 copy-done.1
  11.3 0.0 copy-start
  11.3 1.8 %collective-permute-start.8 = (f32[128,128]{1,0:T(8,128)S(1)}, f32[128,128]{1,0:T(8,128)S(1)}, u32[]{:S(2)}, u32[]{:S(2)}) collective-permute-start(f32[128,128]{1,0:T(8,128)S(1)} %shard_map.48.refs_7_), channel_id=1, source_target_pairs={{0,1},{1,0},{2,3},{3,2},{4,5},{5,4},{6,7},{7,6},{8,9},{9,8},{10,11... | collective-permute-start | bytes 196616 | tf_op jit(solution)/shard_map/ppermute | solution.py:102
  13.1 0.6 %collective-permute-start.7 = (f32[128,128]{1,0:T(8,128)S(1)}, f32[128,128]{1,0:T(8,128)S(1)}, u32[]{:S(2)}, u32[]{:S(2)}) collective-permute-start(f32[128,128]{1,0:T(8,128)S(1)} %shard_map.48.refs_7_), channel_id=1, source_target_pairs={{0,2},{1,3},{2,0},{3,1},{4,6},{5,7},{6,4},{7,5},{8,10},{9,11},{10,... | collective-permute-start | bytes 196616 | tf_op jit(solution)/shard_map/ppermute | solution.py:102
  13.6 2.1 %collective-permute-start.6 = (f32[128,128]{1,0:T(8,128)S(1)}, f32[128,128]{1,0:T(8,128)S(1)}, u32[]{:S(2)}, u32[]{:S(2)}) collective-permute-start(f32[128,128]{1,0:T(8,128)S(1)} %shard_map.48.refs_7_), channel_id=1, source_target_pairs={{0,3},{1,2},{2,1},{3,0},{4,7},{5,6},{6,5},{7,4},{8,11},{9,10},{10,... | collective-permute-start | bytes 196616 | tf_op jit(solution)/shard_map/ppermute | solution.py:102
  15.8 0.0 collective-permute-done.1.refs_2_
  15.8 0.0 collective-permute-done.2.refs_3_
  15.8 2.5 %collective-permute-start.5 = (f32[200,128]{1,0:T(8,128)S(1)}, f32[200,128]{1,0:T(8,128)S(1)}, u32[]{:S(2)}, u32[]{:S(2)}) collective-permute-start(f32[200,128]{1,0:T(8,128)S(1)} %constant_dynamic-update-slice_fusion.refs_0_), channel_id=1, source_target_pairs={{0,24},{4,28},{8,16},{12,20},{16,8},{20,12},{24,0},{28,4},{1,25},{... | collective-permute-start | bytes 307208 | tf_op jit(solution)/shard_map/ppermute | solution.py:102
  18.3 0.5 %collective-permute-start.4 = (f32[200,128]{1,0:T(8,128)S(1)}, f32[200,128]{1,0:T(8,128)S(1)}, u32[]{:S(2)}, u32[]{:S(2)}) collective-permute-start(f32[200,128]{1,0:T(8,128)S(1)} %constant_dynamic-update-slice_fusion.refs_0_), channel_id=1, source_target_pairs={{0,16},{4,20},{8,24},{12,28},{16,0},{20,4},{24,8},{28,12},{1,17},{... | collective-permute-start | bytes 307208 | tf_op jit(solution)/shard_map/ppermute | solution.py:102
  18.8 0.0 collective-permute-done.8.refs_6_
  18.8 0.5 %collective-permute-start.3 = (f32[200,128]{1,0:T(8,128)S(1)}, f32[200,128]{1,0:T(8,128)S(1)}, u32[]{:S(2)}, u32[]{:S(2)}) collective-permute-start(f32[200,128]{1,0:T(8,128)S(1)} %constant_dynamic-update-slice_fusion.refs_0_), channel_id=1, source_target_pairs={{0,8},{4,12},{8,0},{12,4},{16,24},{20,28},{24,16},{28,20},{1,9},{5... | collective-permute-start | bytes 307208 | tf_op jit(solution)/shard_map/ppermute | solution.py:102
  19.4 0.0 collective-permute-done.7.refs_5_
  19.4 0.4 %collective-permute-done.6.refs_4_ = f32[128,128]{1,0:T(8,128)S(1)} collective-permute-done((f32[128,128]{1,0:T(8,128)S(1)}, f32[128,128]{1,0:T(8,128)S(1)}, u32[]{:S(2)}, u32[]{:S(2)}) %collective-permute-start.6) | collective-permute-done | bytes 65568 | tf_op jit(solution)/shard_map/ppermute | solution.py:102
  19.8 0.0 copy-done
  19.8 0.1 shard_map.49.group_ref
  19.9 0.1 collective-permute-start.9
  20.0 0.3 shard_map.50
  20.3 2.2 %collective-permute-done.5.refs_3_ = f32[200,128]{1,0:T(8,128)S(1)} collective-permute-done((f32[200,128]{1,0:T(8,128)S(1)}, f32[200,128]{1,0:T(8,128)S(1)}, u32[]{:S(2)}, u32[]{:S(2)}) %collective-permute-start.5) | collective-permute-done | bytes 102432 | tf_op jit(solution)/shard_map/ppermute | solution.py:102
  22.4 0.9 %collective-permute-done.4.refs_2_ = f32[200,128]{1,0:T(8,128)S(1)} collective-permute-done((f32[200,128]{1,0:T(8,128)S(1)}, f32[200,128]{1,0:T(8,128)S(1)}, u32[]{:S(2)}, u32[]{:S(2)}) %collective-permute-start.4) | collective-permute-done | bytes 102432 | tf_op jit(solution)/shard_map/ppermute | solution.py:102
  23.3 0.2 collective-permute-done.3.refs_1_
  23.5 0.2 shard_map.47
  23.7 0.0 collective-permute-done.9.group_ref
  23.7 0.3 shard_map.51
  24.0 1.9 %shard_map.52 = (f32[128,128]{1,0:T(8,128)S(1)}, f32[128,128]{1,0:T(8,128)S(1)}, f32[128,128]{1,0:T(8,128)S(1)}, f32[128,128]{1,0:T(8,128)S(1)}) custom-call(bf16[576,512]{1,0:T(8,128)(2,1)S(1)} %get-tuple-element.16.row_ref, f32[1,512]{1,0:T(1,128)S(1)} %get-tuple-element.17.scale_ref, f32[8,512]{1,0:T(8,128)S(1)} %get-tuple-element.18.mask_ref, ...), custom_call_target="tpu_custom_call" | custom-call | tf_op jit(solution)/shard_map/pallas_call | solution.py:170
  25.9 1.6 %collective-permute-start.10 = (f32[128,128]{1,0:T(8,128)S(1)}, f32[128,128]{1,0:T(8,128)S(1)}, u32[]{:S(2)}, u32[]{:S(2)}) collective-permute-start(f32[128,128]{1,0:T(8,128)S(1)} %get-tuple-element.24), channel_id=1, source_target_pairs={{0,24},{4,28},{8,16},{12,20},{16,8},{20,12},{24,0},{28,4},{1,25},{... | collective-permute-start | bytes 196616 | tf_op jit(solution)/shard_map/ppermute | solution.py:102
  27.4 0.6 %collective-permute-start.11 = (f32[128,128]{1,0:T(8,128)S(1)}, f32[128,128]{1,0:T(8,128)S(1)}, u32[]{:S(2)}, u32[]{:S(2)}) collective-permute-start(f32[128,128]{1,0:T(8,128)S(1)} %get-tuple-element.25), channel_id=1, source_target_pairs={{0,16},{4,20},{8,24},{12,28},{16,0},{20,4},{24,8},{28,12},{1,17},{... | collective-permute-start | bytes 196616 | tf_op jit(solution)/shard_map/ppermute | solution.py:102
  28.0 1.4 %collective-permute-start.12 = (f32[128,128]{1,0:T(8,128)S(1)}, f32[128,128]{1,0:T(8,128)S(1)}, u32[]{:S(2)}, u32[]{:S(2)}) collective-permute-start(f32[128,128]{1,0:T(8,128)S(1)} %get-tuple-element.26), channel_id=1, source_target_pairs={{0,8},{4,12},{8,0},{12,4},{16,24},{20,28},{24,16},{28,20},{1,9},{5... | collective-permute-start | bytes 196616 | tf_op jit(solution)/shard_map/ppermute | solution.py:102
  29.4 2.1 %collective-permute-done.10 = f32[128,128]{1,0:T(8,128)S(1)} collective-permute-done((f32[128,128]{1,0:T(8,128)S(1)}, f32[128,128]{1,0:T(8,128)S(1)}, u32[]{:S(2)}, u32[]{:S(2)}) %collective-permute-start.10) | collective-permute-done | bytes 65568 | tf_op jit(solution)/shard_map/ppermute | solution.py:102
  31.5 0.4 %collective-permute-done.11 = f32[128,128]{1,0:T(8,128)S(1)} collective-permute-done((f32[128,128]{1,0:T(8,128)S(1)}, f32[128,128]{1,0:T(8,128)S(1)}, u32[]{:S(2)}, u32[]{:S(2)}) %collective-permute-start.11) | collective-permute-done | bytes 65568 | tf_op jit(solution)/shard_map/ppermute | solution.py:102
  32.0 0.3 collective-permute-done.12
  32.3 0.6 %add_add_fusion = f32[128,128]{1,0:T(8,128)} fusion(f32[128,128]{1,0:T(8,128)S(1)} %collective-permute-done.12, f32[128,128]{1,0:T(8,128)S(1)} %collective-permute-done.11, f32[128,128]{1,0:T(8,128)S(1)} %get-tuple-element.23, f32[128,128]{1,0:T(8,128)S(1)} %collective-permute-done.10), kind=kLoop, calls=%fused_computation | loop fusion | flops 49152 | bytes 327680 | tf_op jit(solution)/shard_map/add | solution.py:177
  (5 shorter events, 0.0 us)
Async XLA Ops:
  0.0 11.3 %copy-start.1 = (f32[128,128]{1,0:T(8,128)S(1)}, f32[128,128]{1,0:T(8,128)}, u32[]{:S(2)}) copy-start(f32[128,128]{1,0:T(8,128)} %in_ref.1) | copy-start | bytes 196612
  0.0 15.8 %collective-permute-start.1 = (f32[48,512]{1,0:T(8,128)}, f32[48,512]{1,0:T(8,128)S(1)}, u32[]{:S(2)}, u32[]{:S(2)}) collective-permute-start(f32[48,512]{1,0:T(8,128)} %refs_0_.1), channel_id=1, source_target_pairs={{0,3},{1,2},{2,1},{3,0},{4,7},{5,6},{6,5},{7,4},{8,11},{9,10},{10,... | collective-permute-start | bytes 294920 | tf_op jit(solution)/shard_map/ppermute | solution.py:102
  5.1 6.2 %collective-permute-start = (f32[48,512]{1,0:T(8,128)}, f32[48,512]{1,0:T(8,128)S(1)}, u32[]{:S(2)}, u32[]{:S(2)}) collective-permute-start(f32[48,512]{1,0:T(8,128)} %refs_0_.1), channel_id=1, source_target_pairs={{0,1},{1,0},{2,3},{3,2},{4,5},{5,4},{6,7},{7,6},{8,9},{9,8},{10,11... | collective-permute-start | bytes 294920 | tf_op jit(solution)/shard_map/ppermute | solution.py:102
  5.1 10.7 %collective-permute-start.2 = (f32[48,512]{1,0:T(8,128)}, f32[48,512]{1,0:T(8,128)S(1)}, u32[]{:S(2)}, u32[]{:S(2)}) collective-permute-start(f32[48,512]{1,0:T(8,128)} %refs_0_.1), channel_id=1, source_target_pairs={{0,2},{1,3},{2,0},{3,1},{4,6},{5,7},{6,4},{7,5},{8,10},{9,11},{10,... | collective-permute-start | bytes 294920 | tf_op jit(solution)/shard_map/ppermute | solution.py:102
  5.7 0.7 %copy-start.2 = (s32[4,8]{1,0:T(4,128)S(1)}, s32[4,8]{1,0:T(4,128)}, u32[]{:S(2)}) copy-start(s32[4,8]{1,0:T(4,128)} %list_ref.1) | copy-start | bytes 388
  6.4 0.7 %copy-start.3 = (s32[4]{0:T(128)S(1)}, s32[4]{0:T(128)}, u32[]{:S(2)}) copy-start(s32[4]{0:T(128)} %count_ref.1) | copy-start | bytes 52
  11.3 8.5 %copy-start = (f32[48,512]{1,0:T(8,128)S(1)}, f32[48,512]{1,0:T(8,128)}, u32[]{:S(2)}) copy-start(f32[48,512]{1,0:T(8,128)} %refs_0_.1) | copy-start | bytes 294916
  11.3 7.5 %collective-permute-start.8 = (f32[128,128]{1,0:T(8,128)S(1)}, f32[128,128]{1,0:T(8,128)S(1)}, u32[]{:S(2)}, u32[]{:S(2)}) collective-permute-start(f32[128,128]{1,0:T(8,128)S(1)} %shard_map.48.refs_7_), channel_id=1, source_target_pairs={{0,1},{1,0},{2,3},{3,2},{4,5},{5,4},{6,7},{7,6},{8,9},{9,8},{10,11... | collective-permute-start | bytes 196616 | tf_op jit(solution)/shard_map/ppermute | solution.py:102
  13.1 6.3 %collective-permute-start.7 = (f32[128,128]{1,0:T(8,128)S(1)}, f32[128,128]{1,0:T(8,128)S(1)}, u32[]{:S(2)}, u32[]{:S(2)}) collective-permute-start(f32[128,128]{1,0:T(8,128)S(1)} %shard_map.48.refs_7_), channel_id=1, source_target_pairs={{0,2},{1,3},{2,0},{3,1},{4,6},{5,7},{6,4},{7,5},{8,10},{9,11},{10,... | collective-permute-start | bytes 196616 | tf_op jit(solution)/shard_map/ppermute | solution.py:102
  13.6 6.2 %collective-permute-start.6 = (f32[128,128]{1,0:T(8,128)S(1)}, f32[128,128]{1,0:T(8,128)S(1)}, u32[]{:S(2)}, u32[]{:S(2)}) collective-permute-start(f32[128,128]{1,0:T(8,128)S(1)} %shard_map.48.refs_7_), channel_id=1, source_target_pairs={{0,3},{1,2},{2,1},{3,0},{4,7},{5,6},{6,5},{7,4},{8,11},{9,10},{10,... | collective-permute-start | bytes 196616 | tf_op jit(solution)/shard_map/ppermute | solution.py:102
  15.8 6.6 %collective-permute-start.5 = (f32[200,128]{1,0:T(8,128)S(1)}, f32[200,128]{1,0:T(8,128)S(1)}, u32[]{:S(2)}, u32[]{:S(2)}) collective-permute-start(f32[200,128]{1,0:T(8,128)S(1)} %constant_dynamic-update-slice_fusion.refs_0_), channel_id=1, source_target_pairs={{0,24},{4,28},{8,16},{12,20},{16,8},{20,12},{24,0},{28,4},{1,25},{... | collective-permute-start | bytes 307208 | tf_op jit(solution)/shard_map/ppermute | solution.py:102
  18.3 5.0 %collective-permute-start.4 = (f32[200,128]{1,0:T(8,128)S(1)}, f32[200,128]{1,0:T(8,128)S(1)}, u32[]{:S(2)}, u32[]{:S(2)}) collective-permute-start(f32[200,128]{1,0:T(8,128)S(1)} %constant_dynamic-update-slice_fusion.refs_0_), channel_id=1, source_target_pairs={{0,16},{4,20},{8,24},{12,28},{16,0},{20,4},{24,8},{28,12},{1,17},{... | collective-permute-start | bytes 307208 | tf_op jit(solution)/shard_map/ppermute | solution.py:102
  18.8 4.7 %collective-permute-start.3 = (f32[200,128]{1,0:T(8,128)S(1)}, f32[200,128]{1,0:T(8,128)S(1)}, u32[]{:S(2)}, u32[]{:S(2)}) collective-permute-start(f32[200,128]{1,0:T(8,128)S(1)} %constant_dynamic-update-slice_fusion.refs_0_), channel_id=1, source_target_pairs={{0,8},{4,12},{8,0},{12,4},{16,24},{20,28},{24,16},{28,20},{1,9},{5... | collective-permute-start | bytes 307208 | tf_op jit(solution)/shard_map/ppermute | solution.py:102
  19.9 3.8 %collective-permute-start.9 = (f32[320,512]{1,0:T(8,128)S(1)}, f32[320,512]{1,0:T(8,128)S(1)}, u32[]{:S(2)}, u32[]{:S(2)}) collective-permute-start(f32[320,512]{1,0:T(8,128)S(1)} %shard_map.49.group_ref), channel_id=1, source_target_pairs={{0,4},{4,0},{8,12},{12,8},{16,20},{20,16},{24,28},{28,24},{1,5},{5... | collective-permute-start | bytes 1966088 | tf_op jit(solution)/shard_map/ppermute | solution.py:102
  25.9 5.7 %collective-permute-start.10 = (f32[128,128]{1,0:T(8,128)S(1)}, f32[128,128]{1,0:T(8,128)S(1)}, u32[]{:S(2)}, u32[]{:S(2)}) collective-permute-start(f32[128,128]{1,0:T(8,128)S(1)} %get-tuple-element.24), channel_id=1, source_target_pairs={{0,24},{4,28},{8,16},{12,20},{16,8},{20,12},{24,0},{28,4},{1,25},{... | collective-permute-start | bytes 196616 | tf_op jit(solution)/shard_map/ppermute | solution.py:102
  27.4 4.6 %collective-permute-start.11 = (f32[128,128]{1,0:T(8,128)S(1)}, f32[128,128]{1,0:T(8,128)S(1)}, u32[]{:S(2)}, u32[]{:S(2)}) collective-permute-start(f32[128,128]{1,0:T(8,128)S(1)} %get-tuple-element.25), channel_id=1, source_target_pairs={{0,16},{4,20},{8,24},{12,28},{16,0},{20,4},{24,8},{28,12},{1,17},{... | collective-permute-start | bytes 196616 | tf_op jit(solution)/shard_map/ppermute | solution.py:102
  28.0 4.3 %collective-permute-start.12 = (f32[128,128]{1,0:T(8,128)S(1)}, f32[128,128]{1,0:T(8,128)S(1)}, u32[]{:S(2)}, u32[]{:S(2)}) collective-permute-start(f32[128,128]{1,0:T(8,128)S(1)} %get-tuple-element.26), channel_id=1, source_target_pairs={{0,8},{4,12},{8,0},{12,4},{16,24},{20,28},{24,16},{28,20},{1,9},{5... | collective-permute-start | bytes 196616 | tf_op jit(solution)/shard_map/ppermute | solution.py:102
where the time goes:
time: 33.1 us; the launch traced here: 32.9 us
  starting transfers between devices  17.3 us (52%)
  waiting for transfers between devices  9.47 us (29%)
  Pallas kernels  3.27 us (10%)
  local copies, waits for them, and re-layouts  2.12 us (6%)
  other arithmetic  0.65 us (2%)
    ppermute x13, starting transfers between devices, swapped(): lax.ppermute(value, axis, [(source, source ^ step) for source in range(co...  17.3 us
    ppermute x13, waiting for transfers between devices, swapped(): lax.ppermute(value, axis, [(source, source ^ step) for source in range(co...  9.47 us
    unnamed x12, local copies, waits for them, and re-layouts  2.12 us
    pallas_call x1, Pallas kernels, shards(): pl.pallas_call(apply_kernel, out_shape=[shape((eig_count, width), f32)] *...  1.86 us
  transfers between devices with their start and end apart: 13, of which 8 were waited for; matrix products, arithmetic and copies ran while one was open for 2% of the time, Pallas kernels for 3%

commit v1 on v0

--- a/solution.py
+++ b/solution.py
@@ -128,7 +128,8 @@
         out_shape=shape(eigvecs.shape, f32),
         compiler_params=params,
     )(near, eigvecs)
-    vecs = [swapped(late_vecs, "rep", step) for step in range(rep_size - 1, 0, -1)] + [late_vecs]
+    vecs = [swapped(late_vecs if step > 1 else eigvecs, "rep", step) for step in range(rep_size - 1, 0, -1)]
+    vecs = [*vecs, late_vecs]
     lists = pl.pallas_call(
         lists_kernel,
         in_specs=[smem, smem],

time: 33.1 us -> 32.9 us (level)
  transfers between devices with their start and end apart: 13 -> 13, of which waited for: 8 -> 7; matrix products, arithmetic and copies ran while one was open for 2% -> 2% of each run, Pallas kernels for 3% -> 3%
where the time goes in v1:
time: 32.9 us; the launch traced here: 32.7 us
  starting transfers between devices  17.3 us (53%)
  waiting for transfers between devices  9.23 us (28%)
  Pallas kernels  3.27 us (10%)
  local copies, waits for them, and re-layouts  2.12 us (6%)
  other arithmetic  0.65 us (2%)
    ppermute x13, starting transfers between devices, swapped(): lax.ppermute(value, axis, [(source, source ^ step) for source in range(co...  17.3 us
    ppermute x13, waiting for transfers between devices, swapped(): lax.ppermute(value, axis, [(source, source ^ step) for source in range(co...  9.23 us
    unnamed x12, local copies, waits for them, and re-layouts  2.12 us
    pallas_call x1, Pallas kernels, shards(): pl.pallas_call(apply_kernel, out_shape=[shape((eig_count, width), f32)] *...  1.86 us
  transfers between devices with their start and end apart: 13, of which 7 were waited for; matrix products, arithmetic and copies ran while one was open for 2% of the time, Pallas kernels for 3%

profile of v1, /device:TPU:0, one launch (start us, length us, event | category | flops | bytes accessed | tf_op | source)
XLA Modules:
  0.0 32.7 jit_solution(11429347976253383929)
XLA Ops:
  0.0 0.0 copy-start.1
  0.0 5.0 %collective-permute-start.1 = (f32[48,512]{1,0:T(8,128)}, f32[48,512]{1,0:T(8,128)S(1)}, u32[]{:S(2)}, u32[]{:S(2)}) collective-permute-start(f32[48,512]{1,0:T(8,128)} %refs_0_.1), channel_id=1, source_target_pairs={{0,3},{1,2},{2,1},{3,0},{4,7},{5,6},{6,5},{7,4},{8,11},{9,10},{10,... | collective-permute-start | bytes 294920 | tf_op jit(solution)/shard_map/ppermute | solution.py:102
  5.1 0.0 collective-permute-start
  5.1 0.6 %collective-permute-start.2 = (f32[48,512]{1,0:T(8,128)}, f32[48,512]{1,0:T(8,128)S(1)}, u32[]{:S(2)}, u32[]{:S(2)}) collective-permute-start(f32[48,512]{1,0:T(8,128)} %refs_0_.1), channel_id=1, source_target_pairs={{0,2},{1,3},{2,0},{3,1},{4,6},{5,7},{6,4},{7,5},{8,10},{9,11},{10,... | collective-permute-start | bytes 294920 | tf_op jit(solution)/shard_map/ppermute | solution.py:102
  5.7 1.4 %collective-permute-start.8 = (f32[128,128]{1,0:T(8,128)}, f32[128,128]{1,0:T(8,128)S(1)}, u32[]{:S(2)}, u32[]{:S(2)}) collective-permute-start(f32[128,128]{1,0:T(8,128)} %in_ref.1), channel_id=1, source_target_pairs={{0,1},{1,0},{2,3},{3,2},{4,5},{5,4},{6,7},{7,6},{8,9},{9,8},{10,11... | collective-permute-start | bytes 196616 | tf_op jit(solution)/shard_map/ppermute | solution.py:102
  7.1 0.0 copy-start.2
  7.1 0.7 %copy-done.2 = s32[4,8]{1,0:T(4,128)S(1)} copy-done((s32[4,8]{1,0:T(4,128)S(1)}, s32[4,8]{1,0:T(4,128)}, u32[]{:S(2)}) %copy-start.2) | copy-done | bytes 152
  7.8 0.0 copy-start.3
  7.8 0.7 %copy-done.3 = s32[4]{0:T(128)S(1)} copy-done((s32[4]{0:T(128)S(1)}, s32[4]{0:T(128)}, u32[]{:S(2)}) %copy-start.3) | copy-done | bytes 40
  8.4 0.6 %shard_map.46 = f32[8,128]{1,0:T(8,128)S(1)} custom-call(s32[4,8]{1,0:T(4,128)S(1)} %copy-done.2, s32[4]{0:T(128)S(1)} %copy-done.3), custom_call_target="tpu_custom_call" | custom-call | tf_op jit(solution)/shard_map/pallas_call | solution.py:133
  9.0 0.7 %dynamic-slice_dynamic-update-slice_fusion.3 = f32[200,128]{1,0:T(8,128)S(1)} fusion(f32[48,512]{1,0:T(8,128)} %refs_0_.1, s32[]{:T(128)S(6)} %select_n.2), kind=kLoop, calls=%fused_computation.4 | loop fusion | bytes 49156
  9.8 2.7 %collective-permute-done.before_ref.refs_1_ = f32[48,512]{1,0:T(8,128)S(1)} collective-permute-done((f32[48,512]{1,0:T(8,128)}, f32[48,512]{1,0:T(8,128)S(1)}, u32[]{:S(2)}, u32[]{:S(2)}) %collective-permute-start) | collective-permute-done | bytes 98336 | tf_op jit(solution)/shard_map/ppermute | solution.py:102
  12.4 0.0 copy-done.1
  12.5 0.0 copy-start
  12.5 0.3 collective-permute-start.7
  12.8 2.7 %collective-permute-start.6 = (f32[128,128]{1,0:T(8,128)S(1)}, f32[128,128]{1,0:T(8,128)S(1)}, u32[]{:S(2)}, u32[]{:S(2)}) collective-permute-start(f32[128,128]{1,0:T(8,128)S(1)} %shard_map.48.refs_7_), channel_id=1, source_target_pairs={{0,3},{1,2},{2,1},{3,0},{4,7},{5,6},{6,5},{7,4},{8,11},{9,10},{10,... | collective-permute-start | bytes 196616 | tf_op jit(solution)/shard_map/ppermute | solution.py:102
  15.5 0.0 collective-permute-done.1.refs_2_
  15.5 0.0 collective-permute-done.2.refs_3_
  15.6 2.5 %collective-permute-start.5 = (f32[200,128]{1,0:T(8,128)S(1)}, f32[200,128]{1,0:T(8,128)S(1)}, u32[]{:S(2)}, u32[]{:S(2)}) collective-permute-start(f32[200,128]{1,0:T(8,128)S(1)} %constant_dynamic-update-slice_fusion.refs_0_), channel_id=1, source_target_pairs={{0,24},{4,28},{8,16},{12,20},{16,8},{20,12},{24,0},{28,4},{1,25},{... | collective-permute-start | bytes 307208 | tf_op jit(solution)/shard_map/ppermute | solution.py:102
  18.1 0.5 %collective-permute-start.4 = (f32[200,128]{1,0:T(8,128)S(1)}, f32[200,128]{1,0:T(8,128)S(1)}, u32[]{:S(2)}, u32[]{:S(2)}) collective-permute-start(f32[200,128]{1,0:T(8,128)S(1)} %constant_dynamic-update-slice_fusion.refs_0_), channel_id=1, source_target_pairs={{0,16},{4,20},{8,24},{12,28},{16,0},{20,4},{24,8},{28,12},{1,17},{... | collective-permute-start | bytes 307208 | tf_op jit(solution)/shard_map/ppermute | solution.py:102
  18.6 0.0 collective-permute-done.8.refs_6_
  18.6 0.5 %collective-permute-start.3 = (f32[200,128]{1,0:T(8,128)S(1)}, f32[200,128]{1,0:T(8,128)S(1)}, u32[]{:S(2)}, u32[]{:S(2)}) collective-permute-start(f32[200,128]{1,0:T(8,128)S(1)} %constant_dynamic-update-slice_fusion.refs_0_), channel_id=1, source_target_pairs={{0,8},{4,12},{8,0},{12,4},{16,24},{20,28},{24,16},{28,20},{1,9},{5... | collective-permute-start | bytes 307208 | tf_op jit(solution)/shard_map/ppermute | solution.py:102
  19.1 0.0 collective-permute-done.7.refs_5_
  19.1 0.0 collective-permute-done.6.refs_4_
  19.1 0.0 copy-done
  19.1 0.1 shard_map.49.group_ref
  19.2 0.1 collective-permute-start.9
  19.3 0.3 shard_map.50
  19.6 1.6 %collective-permute-done.5.refs_3_ = f32[200,128]{1,0:T(8,128)S(1)} collective-permute-done((f32[200,128]{1,0:T(8,128)S(1)}, f32[200,128]{1,0:T(8,128)S(1)}, u32[]{:S(2)}, u32[]{:S(2)}) %collective-permute-start.5) | collective-permute-done | bytes 102432 | tf_op jit(solution)/shard_map/ppermute | solution.py:102
  21.2 1.5 %collective-permute-done.4.refs_2_ = f32[200,128]{1,0:T(8,128)S(1)} collective-permute-done((f32[200,128]{1,0:T(8,128)S(1)}, f32[200,128]{1,0:T(8,128)S(1)}, u32[]{:S(2)}, u32[]{:S(2)}) %collective-permute-start.4) | collective-permute-done | bytes 102432 | tf_op jit(solution)/shard_map/ppermute | solution.py:102
  22.7 0.5 %collective-permute-done.3.refs_1_ = f32[200,128]{1,0:T(8,128)S(1)} collective-permute-done((f32[200,128]{1,0:T(8,128)S(1)}, f32[200,128]{1,0:T(8,128)S(1)}, u32[]{:S(2)}, u32[]{:S(2)}) %collective-permute-start.3) | collective-permute-done | bytes 102432 | tf_op jit(solution)/shard_map/ppermute | solution.py:102
  23.3 0.2 shard_map.47
  23.4 0.0 collective-permute-done.9.group_ref
  23.4 0.3 shard_map.51
  23.7 1.9 %shard_map.52 = (f32[128,128]{1,0:T(8,128)S(1)}, f32[128,128]{1,0:T(8,128)S(1)}, f32[128,128]{1,0:T(8,128)S(1)}, f32[128,128]{1,0:T(8,128)S(1)}) custom-call(bf16[576,512]{1,0:T(8,128)(2,1)S(1)} %get-tuple-element.16.row_ref, f32[1,512]{1,0:T(1,128)S(1)} %get-tuple-element.17.scale_ref, f32[8,512]{1,0:T(8,128)S(1)} %get-tuple-element.18.mask_ref, ...), custom_call_target="tpu_custom_call" | custom-call | tf_op jit(solution)/shard_map/pallas_call | solution.py:171
  25.6 1.6 %collective-permute-start.10 = (f32[128,128]{1,0:T(8,128)S(1)}, f32[128,128]{1,0:T(8,128)S(1)}, u32[]{:S(2)}, u32[]{:S(2)}) collective-permute-start(f32[128,128]{1,0:T(8,128)S(1)} %get-tuple-element.24), channel_id=1, source_target_pairs={{0,24},{4,28},{8,16},{12,20},{16,8},{20,12},{24,0},{28,4},{1,25},{... | collective-permute-start | bytes 196616 | tf_op jit(solution)/shard_map/ppermute | solution.py:102
  27.2 0.6 %collective-permute-start.11 = (f32[128,128]{1,0:T(8,128)S(1)}, f32[128,128]{1,0:T(8,128)S(1)}, u32[]{:S(2)}, u32[]{:S(2)}) collective-permute-start(f32[128,128]{1,0:T(8,128)S(1)} %get-tuple-element.25), channel_id=1, source_target_pairs={{0,16},{4,20},{8,24},{12,28},{16,0},{20,4},{24,8},{28,12},{1,17},{... | collective-permute-start | bytes 196616 | tf_op jit(solution)/shard_map/ppermute | solution.py:102
  27.8 1.4 %collective-permute-start.12 = (f32[128,128]{1,0:T(8,128)S(1)}, f32[128,128]{1,0:T(8,128)S(1)}, u32[]{:S(2)}, u32[]{:S(2)}) collective-permute-start(f32[128,128]{1,0:T(8,128)S(1)} %get-tuple-element.26), channel_id=1, source_target_pairs={{0,8},{4,12},{8,0},{12,4},{16,24},{20,28},{24,16},{28,20},{1,9},{5... | collective-permute-start | bytes 196616 | tf_op jit(solution)/shard_map/ppermute | solution.py:102
  29.2 2.0 %collective-permute-done.10 = f32[128,128]{1,0:T(8,128)S(1)} collective-permute-done((f32[128,128]{1,0:T(8,128)S(1)}, f32[128,128]{1,0:T(8,128)S(1)}, u32[]{:S(2)}, u32[]{:S(2)}) %collective-permute-start.10) | collective-permute-done | bytes 65568 | tf_op jit(solution)/shard_map/ppermute | solution.py:102
  31.1 0.7 %collective-permute-done.11 = f32[128,128]{1,0:T(8,128)S(1)} collective-permute-done((f32[128,128]{1,0:T(8,128)S(1)}, f32[128,128]{1,0:T(8,128)S(1)}, u32[]{:S(2)}, u32[]{:S(2)}) %collective-permute-start.11) | collective-permute-done | bytes 65568 | tf_op jit(solution)/shard_map/ppermute | solution.py:102
  31.8 0.2 collective-permute-done.12
  32.0 0.6 %add_add_fusion = f32[128,128]{1,0:T(8,128)} fusion(f32[128,128]{1,0:T(8,128)S(1)} %collective-permute-done.12, f32[128,128]{1,0:T(8,128)S(1)} %collective-permute-done.11, f32[128,128]{1,0:T(8,128)S(1)} %get-tuple-element.23, f32[128,128]{1,0:T(8,128)S(1)} %collective-permute-done.10), kind=kLoop, calls=%fused_computation | loop fusion | flops 49152 | bytes 327680 | tf_op jit(solution)/shard_map/add | solution.py:178
  (5 shorter events, 0.0 us)
Async XLA Ops:
  0.0 12.4 %copy-start.1 = (f32[128,128]{1,0:T(8,128)S(1)}, f32[128,128]{1,0:T(8,128)}, u32[]{:S(2)}) copy-start(f32[128,128]{1,0:T(8,128)} %in_ref.1) | copy-start | bytes 196612
  0.0 15.5 %collective-permute-start.1 = (f32[48,512]{1,0:T(8,128)}, f32[48,512]{1,0:T(8,128)S(1)}, u32[]{:S(2)}, u32[]{:S(2)}) collective-permute-start(f32[48,512]{1,0:T(8,128)} %refs_0_.1), channel_id=1, source_target_pairs={{0,3},{1,2},{2,1},{3,0},{4,7},{5,6},{6,5},{7,4},{8,11},{9,10},{10,... | collective-permute-start | bytes 294920 | tf_op jit(solution)/shard_map/ppermute | solution.py:102
  5.1 7.4 %collective-permute-start = (f32[48,512]{1,0:T(8,128)}, f32[48,512]{1,0:T(8,128)S(1)}, u32[]{:S(2)}, u32[]{:S(2)}) collective-permute-start(f32[48,512]{1,0:T(8,128)} %refs_0_.1), channel_id=1, source_target_pairs={{0,1},{1,0},{2,3},{3,2},{4,5},{5,4},{6,7},{7,6},{8,9},{9,8},{10,11... | collective-permute-start | bytes 294920 | tf_op jit(solution)/shard_map/ppermute | solution.py:102
  5.1 10.5 %collective-permute-start.2 = (f32[48,512]{1,0:T(8,128)}, f32[48,512]{1,0:T(8,128)S(1)}, u32[]{:S(2)}, u32[]{:S(2)}) collective-permute-start(f32[48,512]{1,0:T(8,128)} %refs_0_.1), channel_id=1, source_target_pairs={{0,2},{1,3},{2,0},{3,1},{4,6},{5,7},{6,4},{7,5},{8,10},{9,11},{10,... | collective-permute-start | bytes 294920 | tf_op jit(solution)/shard_map/ppermute | solution.py:102
  5.7 12.9 %collective-permute-start.8 = (f32[128,128]{1,0:T(8,128)}, f32[128,128]{1,0:T(8,128)S(1)}, u32[]{:S(2)}, u32[]{:S(2)}) collective-permute-start(f32[128,128]{1,0:T(8,128)} %in_ref.1), channel_id=1, source_target_pairs={{0,1},{1,0},{2,3},{3,2},{4,5},{5,4},{6,7},{7,6},{8,9},{9,8},{10,11... | collective-permute-start | bytes 196616 | tf_op jit(solution)/shard_map/ppermute | solution.py:102
  7.1 0.7 %copy-start.2 = (s32[4,8]{1,0:T(4,128)S(1)}, s32[4,8]{1,0:T(4,128)}, u32[]{:S(2)}) copy-start(s32[4,8]{1,0:T(4,128)} %list_ref.1) | copy-start | bytes 388
  7.8 0.7 %copy-start.3 = (s32[4]{0:T(128)S(1)}, s32[4]{0:T(128)}, u32[]{:S(2)}) copy-start(s32[4]{0:T(128)} %count_ref.1) | copy-start | bytes 52
  12.5 6.7 %copy-start = (f32[48,512]{1,0:T(8,128)S(1)}, f32[48,512]{1,0:T(8,128)}, u32[]{:S(2)}) copy-start(f32[48,512]{1,0:T(8,128)} %refs_0_.1) | copy-start | bytes 294916
  12.5 6.7 %collective-permute-start.7 = (f32[128,128]{1,0:T(8,128)S(1)}, f32[128,128]{1,0:T(8,128)S(1)}, u32[]{:S(2)}, u32[]{:S(2)}) collective-permute-start(f32[128,128]{1,0:T(8,128)S(1)} %shard_map.48.refs_7_), channel_id=1, source_target_pairs={{0,2},{1,3},{2,0},{3,1},{4,6},{5,7},{6,4},{7,5},{8,10},{9,11},{10,... | collective-permute-start | bytes 196616 | tf_op jit(solution)/shard_map/ppermute | solution.py:102
  12.8 6.4 %collective-permute-start.6 = (f32[128,128]{1,0:T(8,128)S(1)}, f32[128,128]{1,0:T(8,128)S(1)}, u32[]{:S(2)}, u32[]{:S(2)}) collective-permute-start(f32[128,128]{1,0:T(8,128)S(1)} %shard_map.48.refs_7_), channel_id=1, source_target_pairs={{0,3},{1,2},{2,1},{3,0},{4,7},{5,6},{6,5},{7,4},{8,11},{9,10},{10,... | collective-permute-start | bytes 196616 | tf_op jit(solution)/shard_map/ppermute | solution.py:102
  15.6 5.6 %collective-permute-start.5 = (f32[200,128]{1,0:T(8,128)S(1)}, f32[200,128]{1,0:T(8,128)S(1)}, u32[]{:S(2)}, u32[]{:S(2)}) collective-permute-start(f32[200,128]{1,0:T(8,128)S(1)} %constant_dynamic-update-slice_fusion.refs_0_), channel_id=1, source_target_pairs={{0,24},{4,28},{8,16},{12,20},{16,8},{20,12},{24,0},{28,4},{1,25},{... | collective-permute-start | bytes 307208 | tf_op jit(solution)/shard_map/ppermute | solution.py:102
  18.1 4.7 %collective-permute-start.4 = (f32[200,128]{1,0:T(8,128)S(1)}, f32[200,128]{1,0:T(8,128)S(1)}, u32[]{:S(2)}, u32[]{:S(2)}) collective-permute-start(f32[200,128]{1,0:T(8,128)S(1)} %constant_dynamic-update-slice_fusion.refs_0_), channel_id=1, source_target_pairs={{0,16},{4,20},{8,24},{12,28},{16,0},{20,4},{24,8},{28,12},{1,17},{... | collective-permute-start | bytes 307208 | tf_op jit(solution)/shard_map/ppermute | solution.py:102
  18.6 4.7 %collective-permute-start.3 = (f32[200,128]{1,0:T(8,128)S(1)}, f32[200,128]{1,0:T(8,128)S(1)}, u32[]{:S(2)}, u32[]{:S(2)}) collective-permute-start(f32[200,128]{1,0:T(8,128)S(1)} %constant_dynamic-update-slice_fusion.refs_0_), channel_id=1, source_target_pairs={{0,8},{4,12},{8,0},{12,4},{16,24},{20,28},{24,16},{28,20},{1,9},{5... | collective-permute-start | bytes 307208 | tf_op jit(solution)/shard_map/ppermute | solution.py:102
  19.2 4.2 %collective-permute-start.9 = (f32[320,512]{1,0:T(8,128)S(1)}, f32[320,512]{1,0:T(8,128)S(1)}, u32[]{:S(2)}, u32[]{:S(2)}) collective-permute-start(f32[320,512]{1,0:T(8,128)S(1)} %shard_map.49.group_ref), channel_id=1, source_target_pairs={{0,4},{4,0},{8,12},{12,8},{16,20},{20,16},{24,28},{28,24},{1,5},{5... | collective-permute-start | bytes 1966088 | tf_op jit(solution)/shard_map/ppermute | solution.py:102
  25.6 5.5 %collective-permute-start.10 = (f32[128,128]{1,0:T(8,128)S(1)}, f32[128,128]{1,0:T(8,128)S(1)}, u32[]{:S(2)}, u32[]{:S(2)}) collective-permute-start(f32[128,128]{1,0:T(8,128)S(1)} %get-tuple-element.24), channel_id=1, source_target_pairs={{0,24},{4,28},{8,16},{12,20},{16,8},{20,12},{24,0},{28,4},{1,25},{... | collective-permute-start | bytes 196616 | tf_op jit(solution)/shard_map/ppermute | solution.py:102
  27.2 4.6 %collective-permute-start.11 = (f32[128,128]{1,0:T(8,128)S(1)}, f32[128,128]{1,0:T(8,128)S(1)}, u32[]{:S(2)}, u32[]{:S(2)}) collective-permute-start(f32[128,128]{1,0:T(8,128)S(1)} %get-tuple-element.25), channel_id=1, source_target_pairs={{0,16},{4,20},{8,24},{12,28},{16,0},{20,4},{24,8},{28,12},{1,17},{... | collective-permute-start | bytes 196616 | tf_op jit(solution)/shard_map/ppermute | solution.py:102
  27.8 4.3 %collective-permute-start.12 = (f32[128,128]{1,0:T(8,128)S(1)}, f32[128,128]{1,0:T(8,128)S(1)}, u32[]{:S(2)}, u32[]{:S(2)}) collective-permute-start(f32[128,128]{1,0:T(8,128)S(1)} %get-tuple-element.26), channel_id=1, source_target_pairs={{0,8},{4,12},{8,0},{12,4},{16,24},{20,28},{24,16},{28,20},{1,9},{5... | collective-permute-start | bytes 196616 | tf_op jit(solution)/shard_map/ppermute | solution.py:102

commit v2 on v0

--- a/solution.py
+++ b/solution.py
@@ -118,7 +118,7 @@
     params = pltpu.CompilerParams(vmem_limit_bytes=(8 + group_blocks) * 1024 * 1024)
     hint = pl.CostEstimate(flops=TRANSFER_FLOPS, bytes_accessed=1024 * 1024, transcendentals=0)
 
-    send_order = [1, 3, 2, *range(4, rep_size)]
+    send_order = [3, 1, 2, *range(4, rep_size)]
     pieces = {step: swapped(coords, "rep", step) for step in send_order}
     near = pieces[1]
     pieces = [coords] + [pieces[step] for step in send_order]

time: 33.1 us -> 35.3 us (1.066)
  waiting for transfers between devices: 9.47 us -> 11.8 us
    ppermute x13, waiting for transfers between devices: 9.47 us -> 11.8 us  [swapped(): lax.ppermute(value, axis, [(source, source ^ step) for source in range(co...]
  transfers between devices with their start and end apart: 13 -> 13, of which waited for: 8 -> 7; matrix products, arithmetic and copies ran while one was open for 2% -> 2% of each run, Pallas kernels for 3% -> 3%
where the time goes in v2:
time: 35.3 us; the launch traced here: 35.1 us
  starting transfers between devices  17.2 us (49%)
  waiting for transfers between devices  11.8 us (33%)
  Pallas kernels  3.28 us (9%)
  local copies, waits for them, and re-layouts  2.11 us (6%)
  other arithmetic  0.65 us (2%)
    ppermute x13, starting transfers between devices, swapped(): lax.ppermute(value, axis, [(source, source ^ step) for source in range(co...  17.2 us
    ppermute x13, waiting for transfers between devices, swapped(): lax.ppermute(value, axis, [(source, source ^ step) for source in range(co...  11.8 us
    unnamed x12, local copies, waits for them, and re-layouts  2.11 us
    pallas_call x1, Pallas kernels, shards(): pl.pallas_call(apply_kernel, out_shape=[shape((eig_count, width), f32)] *...  1.86 us
  transfers between devices with their start and end apart: 13, of which 7 were waited for; matrix products, arithmetic and copies ran while one was open for 2% of the time, Pallas kernels for 3%

profile of v2, /device:TPU:0, one launch (start us, length us, event | category | flops | bytes accessed | tf_op | source)
XLA Modules:
  0.0 35.1 jit_solution(11870843111051516233)
XLA Ops:
  0.0 0.0 copy-start.1
  0.0 3.0 %collective-permute-start.1 = (f32[48,512]{1,0:T(8,128)}, f32[48,512]{1,0:T(8,128)S(1)}, u32[]{:S(2)}, u32[]{:S(2)}) collective-permute-start(f32[48,512]{1,0:T(8,128)} %refs_0_.1), channel_id=1, source_target_pairs={{0,1},{1,0},{2,3},{3,2},{4,5},{5,4},{6,7},{7,6},{8,9},{9,8},{10,11... | collective-permute-start | bytes 294920 | tf_op jit(solution)/shard_map/ppermute | solution.py:102
  3.0 2.5 %collective-permute-start = (f32[48,512]{1,0:T(8,128)}, f32[48,512]{1,0:T(8,128)S(1)}, u32[]{:S(2)}, u32[]{:S(2)}) collective-permute-start(f32[48,512]{1,0:T(8,128)} %refs_0_.1), channel_id=1, source_target_pairs={{0,3},{1,2},{2,1},{3,0},{4,7},{5,6},{6,5},{7,4},{8,11},{9,10},{10,... | collective-permute-start | bytes 294920 | tf_op jit(solution)/shard_map/ppermute | solution.py:102
  5.5 0.1 collective-permute-start.2
  5.6 0.0 copy-start.2
  5.6 0.7 %copy-done.2 = s32[4,8]{1,0:T(4,128)S(1)} copy-done((s32[4,8]{1,0:T(4,128)S(1)}, s32[4,8]{1,0:T(4,128)}, u32[]{:S(2)}) %copy-start.2) | copy-done | bytes 152
  6.3 0.0 copy-start.3
  6.3 0.7 %copy-done.3 = s32[4]{0:T(128)S(1)} copy-done((s32[4]{0:T(128)S(1)}, s32[4]{0:T(128)}, u32[]{:S(2)}) %copy-start.3) | copy-done | bytes 40
  7.0 0.6 %shard_map.46 = f32[8,128]{1,0:T(8,128)S(1)} custom-call(s32[4,8]{1,0:T(4,128)S(1)} %copy-done.2, s32[4]{0:T(128)S(1)} %copy-done.3), custom_call_target="tpu_custom_call" | custom-call | tf_op jit(solution)/shard_map/pallas_call | solution.py:132
  7.6 0.7 %dynamic-slice_dynamic-update-slice_fusion.3 = f32[200,128]{1,0:T(8,128)S(1)} fusion(f32[48,512]{1,0:T(8,128)} %refs_0_.1, s32[]{:T(128)S(6)} %select_n.2), kind=kLoop, calls=%fused_computation.4 | loop fusion | bytes 49156
  8.3 0.0 collective-permute-done.1.before_ref.refs_2_
  8.3 0.0 copy-done.1
  8.3 0.0 copy-start
  8.3 1.9 %collective-permute-start.8 = (f32[128,128]{1,0:T(8,128)S(1)}, f32[128,128]{1,0:T(8,128)S(1)}, u32[]{:S(2)}, u32[]{:S(2)}) collective-permute-start(f32[128,128]{1,0:T(8,128)S(1)} %shard_map.48.refs_7_), channel_id=1, source_target_pairs={{0,1},{1,0},{2,3},{3,2},{4,5},{5,4},{6,7},{7,6},{8,9},{9,8},{10,11... | collective-permute-start | bytes 196616 | tf_op jit(solution)/shard_map/ppermute | solution.py:102
  10.2 1.7 %collective-permute-start.7 = (f32[128,128]{1,0:T(8,128)S(1)}, f32[128,128]{1,0:T(8,128)S(1)}, u32[]{:S(2)}, u32[]{:S(2)}) collective-permute-start(f32[128,128]{1,0:T(8,128)S(1)} %shard_map.48.refs_7_), channel_id=1, source_target_pairs={{0,2},{1,3},{2,0},{3,1},{4,6},{5,7},{6,4},{7,5},{8,10},{9,11},{10,... | collective-permute-start | bytes 196616 | tf_op jit(solution)/shard_map/ppermute | solution.py:102
  11.9 0.9 %collective-permute-start.6 = (f32[128,128]{1,0:T(8,128)S(1)}, f32[128,128]{1,0:T(8,128)S(1)}, u32[]{:S(2)}, u32[]{:S(2)}) collective-permute-start(f32[128,128]{1,0:T(8,128)S(1)} %shard_map.48.refs_7_), channel_id=1, source_target_pairs={{0,3},{1,2},{2,1},{3,0},{4,7},{5,6},{6,5},{7,4},{8,11},{9,10},{10,... | collective-permute-start | bytes 196616 | tf_op jit(solution)/shard_map/ppermute | solution.py:102
  12.8 0.0 collective-permute-done.refs_1_
  12.8 5.3 %collective-permute-done.2.refs_3_ = f32[48,512]{1,0:T(8,128)S(1)} collective-permute-done((f32[48,512]{1,0:T(8,128)}, f32[48,512]{1,0:T(8,128)S(1)}, u32[]{:S(2)}, u32[]{:S(2)}) %collective-permute-start.2) | collective-permute-done | bytes 98336 | tf_op jit(solution)/shard_map/ppermute | solution.py:102
  18.1 2.4 %collective-permute-start.5 = (f32[200,128]{1,0:T(8,128)S(1)}, f32[200,128]{1,0:T(8,128)S(1)}, u32[]{:S(2)}, u32[]{:S(2)}) collective-permute-start(f32[200,128]{1,0:T(8,128)S(1)} %constant_dynamic-update-slice_fusion.refs_0_), channel_id=1, source_target_pairs={{0,24},{4,28},{8,16},{12,20},{16,8},{20,12},{24,0},{28,4},{1,25},{... | collective-permute-start | bytes 307208 | tf_op jit(solution)/shard_map/ppermute | solution.py:102
  20.5 0.5 %collective-permute-start.4 = (f32[200,128]{1,0:T(8,128)S(1)}, f32[200,128]{1,0:T(8,128)S(1)}, u32[]{:S(2)}, u32[]{:S(2)}) collective-permute-start(f32[200,128]{1,0:T(8,128)S(1)} %constant_dynamic-update-slice_fusion.refs_0_), channel_id=1, source_target_pairs={{0,16},{4,20},{8,24},{12,28},{16,0},{20,4},{24,8},{28,12},{1,17},{... | collective-permute-start | bytes 307208 | tf_op jit(solution)/shard_map/ppermute | solution.py:102
  21.0 0.0 collective-permute-done.8.refs_6_
  21.0 0.5 %collective-permute-start.3 = (f32[200,128]{1,0:T(8,128)S(1)}, f32[200,128]{1,0:T(8,128)S(1)}, u32[]{:S(2)}, u32[]{:S(2)}) collective-permute-start(f32[200,128]{1,0:T(8,128)S(1)} %constant_dynamic-update-slice_fusion.refs_0_), channel_id=1, source_target_pairs={{0,8},{4,12},{8,0},{12,4},{16,24},{20,28},{24,16},{28,20},{1,9},{5... | collective-permute-start | bytes 307208 | tf_op jit(solution)/shard_map/ppermute | solution.py:102
  21.6 0.0 collective-permute-done.7.refs_5_
  21.6 0.0 collective-permute-done.6.refs_4_
  21.6 0.0 copy-done
  21.6 0.1 shard_map.49.group_ref
  21.6 0.1 collective-permute-start.9
  21.7 0.3 shard_map.50
  22.0 1.6 %collective-permute-done.5.refs_3_ = f32[200,128]{1,0:T(8,128)S(1)} collective-permute-done((f32[200,128]{1,0:T(8,128)S(1)}, f32[200,128]{1,0:T(8,128)S(1)}, u32[]{:S(2)}, u32[]{:S(2)}) %collective-permute-start.5) | collective-permute-done | bytes 102432 | tf_op jit(solution)/shard_map/ppermute | solution.py:102
  23.6 1.5 %collective-permute-done.4.refs_2_ = f32[200,128]{1,0:T(8,128)S(1)} collective-permute-done((f32[200,128]{1,0:T(8,128)S(1)}, f32[200,128]{1,0:T(8,128)S(1)}, u32[]{:S(2)}, u32[]{:S(2)}) %collective-permute-start.4) | collective-permute-done | bytes 102432 | tf_op jit(solution)/shard_map/ppermute | solution.py:102
  25.2 0.5 %collective-permute-done.3.refs_1_ = f32[200,128]{1,0:T(8,128)S(1)} collective-permute-done((f32[200,128]{1,0:T(8,128)S(1)}, f32[200,128]{1,0:T(8,128)S(1)}, u32[]{:S(2)}, u32[]{:S(2)}) %collective-permute-start.3) | collective-permute-done | bytes 102432 | tf_op jit(solution)/shard_map/ppermute | solution.py:102
  25.7 0.2 shard_map.47
  25.9 0.0 collective-permute-done.9.group_ref
  25.9 0.3 shard_map.51
  26.2 1.9 %shard_map.52 = (f32[128,128]{1,0:T(8,128)S(1)}, f32[128,128]{1,0:T(8,128)S(1)}, f32[128,128]{1,0:T(8,128)S(1)}, f32[128,128]{1,0:T(8,128)S(1)}) custom-call(bf16[576,512]{1,0:T(8,128)(2,1)S(1)} %get-tuple-element.16.row_ref, f32[1,512]{1,0:T(1,128)S(1)} %get-tuple-element.17.scale_ref, f32[8,512]{1,0:T(8,128)S(1)} %get-tuple-element.18.mask_ref, ...), custom_call_target="tpu_custom_call" | custom-call | tf_op jit(solution)/shard_map/pallas_call | solution.py:170
  28.0 1.6 %collective-permute-start.10 = (f32[128,128]{1,0:T(8,128)S(1)}, f32[128,128]{1,0:T(8,128)S(1)}, u32[]{:S(2)}, u32[]{:S(2)}) collective-permute-start(f32[128,128]{1,0:T(8,128)S(1)} %get-tuple-element.24), channel_id=1, source_target_pairs={{0,24},{4,28},{8,16},{12,20},{16,8},{20,12},{24,0},{28,4},{1,25},{... | collective-permute-start | bytes 196616 | tf_op jit(solution)/shard_map/ppermute | solution.py:102
  29.6 0.6 %collective-permute-start.11 = (f32[128,128]{1,0:T(8,128)S(1)}, f32[128,128]{1,0:T(8,128)S(1)}, u32[]{:S(2)}, u32[]{:S(2)}) collective-permute-start(f32[128,128]{1,0:T(8,128)S(1)} %get-tuple-element.25), channel_id=1, source_target_pairs={{0,16},{4,20},{8,24},{12,28},{16,0},{20,4},{24,8},{28,12},{1,17},{... | collective-permute-start | bytes 196616 | tf_op jit(solution)/shard_map/ppermute | solution.py:102
  30.2 1.4 %collective-permute-start.12 = (f32[128,128]{1,0:T(8,128)S(1)}, f32[128,128]{1,0:T(8,128)S(1)}, u32[]{:S(2)}, u32[]{:S(2)}) collective-permute-start(f32[128,128]{1,0:T(8,128)S(1)} %get-tuple-element.26), channel_id=1, source_target_pairs={{0,8},{4,12},{8,0},{12,4},{16,24},{20,28},{24,16},{28,20},{1,9},{5... | collective-permute-start | bytes 196616 | tf_op jit(solution)/shard_map/ppermute | solution.py:102
  31.6 1.9 %collective-permute-done.10 = f32[128,128]{1,0:T(8,128)S(1)} collective-permute-done((f32[128,128]{1,0:T(8,128)S(1)}, f32[128,128]{1,0:T(8,128)S(1)}, u32[]{:S(2)}, u32[]{:S(2)}) %collective-permute-start.10) | collective-permute-done | bytes 65568 | tf_op jit(solution)/shard_map/ppermute | solution.py:102
  33.5 0.7 %collective-permute-done.11 = f32[128,128]{1,0:T(8,128)S(1)} collective-permute-done((f32[128,128]{1,0:T(8,128)S(1)}, f32[128,128]{1,0:T(8,128)S(1)}, u32[]{:S(2)}, u32[]{:S(2)}) %collective-permute-start.11) | collective-permute-done | bytes 65568 | tf_op jit(solution)/shard_map/ppermute | solution.py:102
  34.2 0.3 collective-permute-done.12
  34.5 0.6 %add_add_fusion = f32[128,128]{1,0:T(8,128)} fusion(f32[128,128]{1,0:T(8,128)S(1)} %collective-permute-done.12, f32[128,128]{1,0:T(8,128)S(1)} %collective-permute-done.11, f32[128,128]{1,0:T(8,128)S(1)} %get-tuple-element.23, f32[128,128]{1,0:T(8,128)S(1)} %collective-permute-done.10), kind=kLoop, calls=%fused_computation | loop fusion | flops 49152 | bytes 327680 | tf_op jit(solution)/shard_map/add | solution.py:177
  (5 shorter events, 0.0 us)
Async XLA Ops:
  0.0 8.3 %copy-start.1 = (f32[128,128]{1,0:T(8,128)S(1)}, f32[128,128]{1,0:T(8,128)}, u32[]{:S(2)}) copy-start(f32[128,128]{1,0:T(8,128)} %in_ref.1) | copy-start | bytes 196612
  0.0 8.3 %collective-permute-start.1 = (f32[48,512]{1,0:T(8,128)}, f32[48,512]{1,0:T(8,128)S(1)}, u32[]{:S(2)}, u32[]{:S(2)}) collective-permute-start(f32[48,512]{1,0:T(8,128)} %refs_0_.1), channel_id=1, source_target_pairs={{0,1},{1,0},{2,3},{3,2},{4,5},{5,4},{6,7},{7,6},{8,9},{9,8},{10,11... | collective-permute-start | bytes 294920 | tf_op jit(solution)/shard_map/ppermute | solution.py:102
  3.0 9.8 %collective-permute-start = (f32[48,512]{1,0:T(8,128)}, f32[48,512]{1,0:T(8,128)S(1)}, u32[]{:S(2)}, u32[]{:S(2)}) collective-permute-start(f32[48,512]{1,0:T(8,128)} %refs_0_.1), channel_id=1, source_target_pairs={{0,3},{1,2},{2,1},{3,0},{4,7},{5,6},{6,5},{7,4},{8,11},{9,10},{10,... | collective-permute-start | bytes 294920 | tf_op jit(solution)/shard_map/ppermute | solution.py:102
  5.5 12.6 %collective-permute-start.2 = (f32[48,512]{1,0:T(8,128)}, f32[48,512]{1,0:T(8,128)S(1)}, u32[]{:S(2)}, u32[]{:S(2)}) collective-permute-start(f32[48,512]{1,0:T(8,128)} %refs_0_.1), channel_id=1, source_target_pairs={{0,2},{1,3},{2,0},{3,1},{4,6},{5,7},{6,4},{7,5},{8,10},{9,11},{10,... | collective-permute-start | bytes 294920 | tf_op jit(solution)/shard_map/ppermute | solution.py:102
  5.6 0.7 %copy-start.2 = (s32[4,8]{1,0:T(4,128)S(1)}, s32[4,8]{1,0:T(4,128)}, u32[]{:S(2)}) copy-start(s32[4,8]{1,0:T(4,128)} %list_ref.1) | copy-start | bytes 388
  6.3 0.7 %copy-start.3 = (s32[4]{0:T(128)S(1)}, s32[4]{0:T(128)}, u32[]{:S(2)}) copy-start(s32[4]{0:T(128)} %count_ref.1) | copy-start | bytes 52
  8.3 13.3 %copy-start = (f32[48,512]{1,0:T(8,128)S(1)}, f32[48,512]{1,0:T(8,128)}, u32[]{:S(2)}) copy-start(f32[48,512]{1,0:T(8,128)} %refs_0_.1) | copy-start | bytes 294916
  8.3 12.7 %collective-permute-start.8 = (f32[128,128]{1,0:T(8,128)S(1)}, f32[128,128]{1,0:T(8,128)S(1)}, u32[]{:S(2)}, u32[]{:S(2)}) collective-permute-start(f32[128,128]{1,0:T(8,128)S(1)} %shard_map.48.refs_7_), channel_id=1, source_target_pairs={{0,1},{1,0},{2,3},{3,2},{4,5},{5,4},{6,7},{7,6},{8,9},{9,8},{10,11... | collective-permute-start | bytes 196616 | tf_op jit(solution)/shard_map/ppermute | solution.py:102
  10.2 11.4 %collective-permute-start.7 = (f32[128,128]{1,0:T(8,128)S(1)}, f32[128,128]{1,0:T(8,128)S(1)}, u32[]{:S(2)}, u32[]{:S(2)}) collective-permute-start(f32[128,128]{1,0:T(8,128)S(1)} %shard_map.48.refs_7_), channel_id=1, source_target_pairs={{0,2},{1,3},{2,0},{3,1},{4,6},{5,7},{6,4},{7,5},{8,10},{9,11},{10,... | collective-permute-start | bytes 196616 | tf_op jit(solution)/shard_map/ppermute | solution.py:102
  11.9 9.7 %collective-permute-start.6 = (f32[128,128]{1,0:T(8,128)S(1)}, f32[128,128]{1,0:T(8,128)S(1)}, u32[]{:S(2)}, u32[]{:S(2)}) collective-permute-start(f32[128,128]{1,0:T(8,128)S(1)} %shard_map.48.refs_7_), channel_id=1, source_target_pairs={{0,3},{1,2},{2,1},{3,0},{4,7},{5,6},{6,5},{7,4},{8,11},{9,10},{10,... | collective-permute-start | bytes 196616 | tf_op jit(solution)/shard_map/ppermute | solution.py:102
  18.1 5.6 %collective-permute-start.5 = (f32[200,128]{1,0:T(8,128)S(1)}, f32[200,128]{1,0:T(8,128)S(1)}, u32[]{:S(2)}, u32[]{:S(2)}) collective-permute-start(f32[200,128]{1,0:T(8,128)S(1)} %constant_dynamic-update-slice_fusion.refs_0_), channel_id=1, source_target_pairs={{0,24},{4,28},{8,16},{12,20},{16,8},{20,12},{24,0},{28,4},{1,25},{... | collective-permute-start | bytes 307208 | tf_op jit(solution)/shard_map/ppermute | solution.py:102
  20.5 4.7 %collective-permute-start.4 = (f32[200,128]{1,0:T(8,128)S(1)}, f32[200,128]{1,0:T(8,128)S(1)}, u32[]{:S(2)}, u32[]{:S(2)}) collective-permute-start(f32[200,128]{1,0:T(8,128)S(1)} %constant_dynamic-update-slice_fusion.refs_0_), channel_id=1, source_target_pairs={{0,16},{4,20},{8,24},{12,28},{16,0},{20,4},{24,8},{28,12},{1,17},{... | collective-permute-start | bytes 307208 | tf_op jit(solution)/shard_map/ppermute | solution.py:102
  21.0 4.7 %collective-permute-start.3 = (f32[200,128]{1,0:T(8,128)S(1)}, f32[200,128]{1,0:T(8,128)S(1)}, u32[]{:S(2)}, u32[]{:S(2)}) collective-permute-start(f32[200,128]{1,0:T(8,128)S(1)} %constant_dynamic-update-slice_fusion.refs_0_), channel_id=1, source_target_pairs={{0,8},{4,12},{8,0},{12,4},{16,24},{20,28},{24,16},{28,20},{1,9},{5... | collective-permute-start | bytes 307208 | tf_op jit(solution)/shard_map/ppermute | solution.py:102
  21.6 4.2 %collective-permute-start.9 = (f32[320,512]{1,0:T(8,128)S(1)}, f32[320,512]{1,0:T(8,128)S(1)}, u32[]{:S(2)}, u32[]{:S(2)}) collective-permute-start(f32[320,512]{1,0:T(8,128)S(1)} %shard_map.49.group_ref), channel_id=1, source_target_pairs={{0,4},{4,0},{8,12},{12,8},{16,20},{20,16},{24,28},{28,24},{1,5},{5... | collective-permute-start | bytes 1966088 | tf_op jit(solution)/shard_map/ppermute | solution.py:102
  28.0 5.5 %collective-permute-start.10 = (f32[128,128]{1,0:T(8,128)S(1)}, f32[128,128]{1,0:T(8,128)S(1)}, u32[]{:S(2)}, u32[]{:S(2)}) collective-permute-start(f32[128,128]{1,0:T(8,128)S(1)} %get-tuple-element.24), channel_id=1, source_target_pairs={{0,24},{4,28},{8,16},{12,20},{16,8},{20,12},{24,0},{28,4},{1,25},{... | collective-permute-start | bytes 196616 | tf_op jit(solution)/shard_map/ppermute | solution.py:102
  29.6 4.6 %collective-permute-start.11 = (f32[128,128]{1,0:T(8,128)S(1)}, f32[128,128]{1,0:T(8,128)S(1)}, u32[]{:S(2)}, u32[]{:S(2)}) collective-permute-start(f32[128,128]{1,0:T(8,128)S(1)} %get-tuple-element.25), channel_id=1, source_target_pairs={{0,16},{4,20},{8,24},{12,28},{16,0},{20,4},{24,8},{28,12},{1,17},{... | collective-permute-start | bytes 196616 | tf_op jit(solution)/shard_map/ppermute | solution.py:102
  30.2 4.3 %collective-permute-start.12 = (f32[128,128]{1,0:T(8,128)S(1)}, f32[128,128]{1,0:T(8,128)S(1)}, u32[]{:S(2)}, u32[]{:S(2)}) collective-permute-start(f32[128,128]{1,0:T(8,128)S(1)} %get-tuple-element.26), channel_id=1, source_target_pairs={{0,8},{4,12},{8,0},{12,4},{16,24},{20,28},{24,16},{28,20},{1,9},{5... | collective-permute-start | bytes 196616 | tf_op jit(solution)/shard_map/ppermute | solution.py:102

commit v3 on v1

--- a/solution.py
+++ b/solution.py
@@ -32,7 +32,7 @@
     out_ref[...] = in_ref[...]
 
 
-def group_kernel(piece_count, *refs):
+def group_kernel(piece_count, order, *refs):
     piece_refs, vec_refs, out_ref = refs[:piece_count], refs[piece_count:-1], refs[-1]
     piece_feats = piece_refs[0].shape[0]
     width = vec_refs[0].shape[1]
@@ -40,7 +40,7 @@
     rank = lax.axis_index("rep")
     for piece, ref in enumerate(piece_refs):
         out_ref[piece * piece_feats : (piece + 1) * piece_feats, :] = ref[...]
-    for spot, ref in enumerate(vec_refs[::-1]):
+    for spot, ref in zip(order, vec_refs):
         span = pl.ds(pl.multiple_of((rank ^ spot) * width, width), width)
         out_ref[feat_count:, span] = ref[...]
 
@@ -128,7 +128,8 @@
         out_shape=shape(eigvecs.shape, f32),
         compiler_params=params,
     )(near, eigvecs)
-    vecs = [swapped(late_vecs if step > 1 else eigvecs, "rep", step) for step in range(rep_size - 1, 0, -1)]
+    order = [*range(2, rep_size), 1, 0]
+    vecs = [swapped(late_vecs if step > 1 else eigvecs, "rep", step) for step in order[:-1]]
     vecs = [*vecs, late_vecs]
     lists = pl.pallas_call(
         lists_kernel,
@@ -143,7 +144,7 @@
     panels = [panel] + [swapped(panel, "blk", step) for step in steps[1:]]
 
     own_group = pl.pallas_call(
-        functools.partial(group_kernel, rep_size),
+        functools.partial(group_kernel, rep_size, order),
         out_shape=shape((feat_count + eig_count, group_cols), f32),
         compiler_params=params,
     )(*pieces, *vecs)

time: 32.9 us -> 32.7 us (level)
  starting transfers between devices: 17.3 us -> 16.4 us
  waiting for transfers between devices: 9.23 us -> 9.98 us
    ppermute x13, starting transfers between devices: 17.3 us -> 16.4 us  [swapped(): lax.ppermute(value, axis, [(source, source ^ step) for source in range(co...]
    ppermute x13, waiting for transfers between devices: 9.23 us -> 9.98 us  [swapped(): lax.ppermute(value, axis, [(source, source ^ step) for source in range(co...]
  transfers between devices with their start and end apart: 13 -> 13, of which waited for: 7 -> 9; matrix products, arithmetic and copies ran while one was open for 2% -> 2% of each run, Pallas kernels for 3% -> 3%
where the time goes in v3:
time: 32.7 us; the launch traced here: 32.5 us
  starting transfers between devices  16.4 us (50%)
  waiting for transfers between devices  9.98 us (31%)
  Pallas kernels  3.26 us (10%)
  local copies, waits for them, and re-layouts  2.12 us (6%)
  other arithmetic  0.65 us (2%)
    ppermute x13, starting transfers between devices, swapped(): lax.ppermute(value, axis, [(source, source ^ step) for source in range(co...  16.4 us
    ppermute x13, waiting for transfers between devices, swapped(): lax.ppermute(value, axis, [(source, source ^ step) for source in range(co...  9.98 us
    unnamed x12, local copies, waits for them, and re-layouts  2.12 us
    pallas_call x1, Pallas kernels, shards(): pl.pallas_call(apply_kernel, out_shape=[shape((eig_count, width), f32)] *...  1.86 us
  transfers between devices with their start and end apart: 13, of which 9 were waited for; matrix products, arithmetic and copies ran while one was open for 2% of the time, Pallas kernels for 3%

profile of v3, /device:TPU:0, one launch (start us, length us, event | category | flops | bytes accessed | tf_op | source)
XLA Modules:
  0.0 32.5 jit_solution(11154451746427778824)
XLA Ops:
  0.0 0.0 copy-start.1
  0.0 5.0 %collective-permute-start.1 = (f32[48,512]{1,0:T(8,128)}, f32[48,512]{1,0:T(8,128)S(1)}, u32[]{:S(2)}, u32[]{:S(2)}) collective-permute-start(f32[48,512]{1,0:T(8,128)} %refs_0_.1), channel_id=1, source_target_pairs={{0,3},{1,2},{2,1},{3,0},{4,7},{5,6},{6,5},{7,4},{8,11},{9,10},{10,... | collective-permute-start | bytes 294920 | tf_op jit(solution)/shard_map/ppermute | solution.py:102
  5.1 0.0 collective-permute-start
  5.1 0.6 %collective-permute-start.2 = (f32[48,512]{1,0:T(8,128)}, f32[48,512]{1,0:T(8,128)S(1)}, u32[]{:S(2)}, u32[]{:S(2)}) collective-permute-start(f32[48,512]{1,0:T(8,128)} %refs_0_.1), channel_id=1, source_target_pairs={{0,2},{1,3},{2,0},{3,1},{4,6},{5,7},{6,4},{7,5},{8,10},{9,11},{10,... | collective-permute-start | bytes 294920 | tf_op jit(solution)/shard_map/ppermute | solution.py:102
  5.7 1.4 %collective-permute-start.8 = (f32[128,128]{1,0:T(8,128)}, f32[128,128]{1,0:T(8,128)S(1)}, u32[]{:S(2)}, u32[]{:S(2)}) collective-permute-start(f32[128,128]{1,0:T(8,128)} %in_ref.1), channel_id=1, source_target_pairs={{0,1},{1,0},{2,3},{3,2},{4,5},{5,4},{6,7},{7,6},{8,9},{9,8},{10,11... | collective-permute-start | bytes 196616 | tf_op jit(solution)/shard_map/ppermute | solution.py:102
  7.1 0.0 copy-start.2
  7.1 0.7 %copy-done.2 = s32[4,8]{1,0:T(4,128)S(1)} copy-done((s32[4,8]{1,0:T(4,128)S(1)}, s32[4,8]{1,0:T(4,128)}, u32[]{:S(2)}) %copy-start.2) | copy-done | bytes 152
  7.8 0.0 copy-start.3
  7.8 0.7 %copy-done.3 = s32[4]{0:T(128)S(1)} copy-done((s32[4]{0:T(128)S(1)}, s32[4]{0:T(128)}, u32[]{:S(2)}) %copy-start.3) | copy-done | bytes 40
  8.4 0.6 %shard_map.46 = f32[8,128]{1,0:T(8,128)S(1)} custom-call(s32[4,8]{1,0:T(4,128)S(1)} %copy-done.2, s32[4]{0:T(128)S(1)} %copy-done.3), custom_call_target="tpu_custom_call" | custom-call | tf_op jit(solution)/shard_map/pallas_call | solution.py:134
  9.0 0.7 %dynamic-slice_dynamic-update-slice_fusion.3 = f32[200,128]{1,0:T(8,128)S(1)} fusion(f32[48,512]{1,0:T(8,128)} %refs_0_.1, s32[]{:T(128)S(6)} %select_n.2), kind=kLoop, calls=%fused_computation.4 | loop fusion | bytes 49156
  9.8 2.7 %collective-permute-done.before_ref.refs_1_ = f32[48,512]{1,0:T(8,128)S(1)} collective-permute-done((f32[48,512]{1,0:T(8,128)}, f32[48,512]{1,0:T(8,128)S(1)}, u32[]{:S(2)}, u32[]{:S(2)}) %collective-permute-start) | collective-permute-done | bytes 98336 | tf_op jit(solution)/shard_map/ppermute | solution.py:102
  12.4 0.0 copy-done.1
  12.5 0.0 copy-start
  12.5 0.9 %collective-permute-start.7 = (f32[128,128]{1,0:T(8,128)S(1)}, f32[128,128]{1,0:T(8,128)S(1)}, u32[]{:S(2)}, u32[]{:S(2)}) collective-permute-start(f32[128,128]{1,0:T(8,128)S(1)} %shard_map.48.refs_7_), channel_id=1, source_target_pairs={{0,3},{1,2},{2,1},{3,0},{4,7},{5,6},{6,5},{7,4},{8,11},{9,10},{10,... | collective-permute-start | bytes 196616 | tf_op jit(solution)/shard_map/ppermute | solution.py:102
  13.3 1.3 %collective-permute-start.6 = (f32[128,128]{1,0:T(8,128)S(1)}, f32[128,128]{1,0:T(8,128)S(1)}, u32[]{:S(2)}, u32[]{:S(2)}) collective-permute-start(f32[128,128]{1,0:T(8,128)S(1)} %shard_map.48.refs_7_), channel_id=1, source_target_pairs={{0,2},{1,3},{2,0},{3,1},{4,6},{5,7},{6,4},{7,5},{8,10},{9,11},{10,... | collective-permute-start | bytes 196616 | tf_op jit(solution)/shard_map/ppermute | solution.py:102
  14.6 0.0 collective-permute-done.1.refs_2_
  14.6 0.0 collective-permute-done.2.refs_3_
  14.7 2.5 %collective-permute-start.5 = (f32[200,128]{1,0:T(8,128)S(1)}, f32[200,128]{1,0:T(8,128)S(1)}, u32[]{:S(2)}, u32[]{:S(2)}) collective-permute-start(f32[200,128]{1,0:T(8,128)S(1)} %constant_dynamic-update-slice_fusion.refs_0_), channel_id=1, source_target_pairs={{0,24},{4,28},{8,16},{12,20},{16,8},{20,12},{24,0},{28,4},{1,25},{... | collective-permute-start | bytes 307208 | tf_op jit(solution)/shard_map/ppermute | solution.py:102
  17.2 0.5 %collective-permute-start.4 = (f32[200,128]{1,0:T(8,128)S(1)}, f32[200,128]{1,0:T(8,128)S(1)}, u32[]{:S(2)}, u32[]{:S(2)}) collective-permute-start(f32[200,128]{1,0:T(8,128)S(1)} %constant_dynamic-update-slice_fusion.refs_0_), channel_id=1, source_target_pairs={{0,16},{4,20},{8,24},{12,28},{16,0},{20,4},{24,8},{28,12},{1,17},{... | collective-permute-start | bytes 307208 | tf_op jit(solution)/shard_map/ppermute | solution.py:102
  17.7 0.0 collective-permute-done.8.refs_6_
  17.7 0.5 %collective-permute-start.3 = (f32[200,128]{1,0:T(8,128)S(1)}, f32[200,128]{1,0:T(8,128)S(1)}, u32[]{:S(2)}, u32[]{:S(2)}) collective-permute-start(f32[200,128]{1,0:T(8,128)S(1)} %constant_dynamic-update-slice_fusion.refs_0_), channel_id=1, source_target_pairs={{0,8},{4,12},{8,0},{12,4},{16,24},{20,28},{24,16},{28,20},{1,9},{5... | collective-permute-start | bytes 307208 | tf_op jit(solution)/shard_map/ppermute | solution.py:102
  18.2 0.5 %collective-permute-done.7.refs_5_ = f32[128,128]{1,0:T(8,128)S(1)} collective-permute-done((f32[128,128]{1,0:T(8,128)S(1)}, f32[128,128]{1,0:T(8,128)S(1)}, u32[]{:S(2)}, u32[]{:S(2)}) %collective-permute-start.7) | collective-permute-done | bytes 65568 | tf_op jit(solution)/shard_map/ppermute | solution.py:102
  18.7 1.2 %collective-permute-done.6.refs_4_ = f32[128,128]{1,0:T(8,128)S(1)} collective-permute-done((f32[128,128]{1,0:T(8,128)S(1)}, f32[128,128]{1,0:T(8,128)S(1)}, u32[]{:S(2)}, u32[]{:S(2)}) %collective-permute-start.6) | collective-permute-done | bytes 65568 | tf_op jit(solution)/shard_map/ppermute | solution.py:102
  19.9 0.0 copy-done
  20.0 0.1 collective-permute-start.9
  20.0 0.3 shard_map.50
  20.3 0.6 %collective-permute-done.5.refs_3_ = f32[200,128]{1,0:T(8,128)S(1)} collective-permute-done((f32[200,128]{1,0:T(8,128)S(1)}, f32[200,128]{1,0:T(8,128)S(1)}, u32[]{:S(2)}, u32[]{:S(2)}) %collective-permute-start.5) | collective-permute-done | bytes 102432 | tf_op jit(solution)/shard_map/ppermute | solution.py:102
  20.9 1.1 %collective-permute-done.4.refs_2_ = f32[200,128]{1,0:T(8,128)S(1)} collective-permute-done((f32[200,128]{1,0:T(8,128)S(1)}, f32[200,128]{1,0:T(8,128)S(1)}, u32[]{:S(2)}, u32[]{:S(2)}) %collective-permute-start.4) | collective-permute-done | bytes 102432 | tf_op jit(solution)/shard_map/ppermute | solution.py:102
  22.0 0.4 %collective-permute-done.3.refs_1_ = f32[200,128]{1,0:T(8,128)S(1)} collective-permute-done((f32[200,128]{1,0:T(8,128)S(1)}, f32[200,128]{1,0:T(8,128)S(1)}, u32[]{:S(2)}, u32[]{:S(2)}) %collective-permute-start.3) | collective-permute-done | bytes 102432 | tf_op jit(solution)/shard_map/ppermute | solution.py:102
  22.4 0.2 shard_map.47
  22.5 0.0 collective-permute-done.9.group_ref
  22.5 0.3 shard_map.51
  22.8 1.9 %shard_map.52 = (f32[128,128]{1,0:T(8,128)S(1)}, f32[128,128]{1,0:T(8,128)S(1)}, f32[128,128]{1,0:T(8,128)S(1)}, f32[128,128]{1,0:T(8,128)S(1)}) custom-call(bf16[576,512]{1,0:T(8,128)(2,1)S(1)} %get-tuple-element.16.row_ref, f32[1,512]{1,0:T(1,128)S(1)} %get-tuple-element.17.scale_ref, f32[8,512]{1,0:T(8,128)S(1)} %get-tuple-element.18.mask_ref, ...), custom_call_target="tpu_custom_call" | custom-call | tf_op jit(solution)/shard_map/pallas_call | solution.py:172
  24.7 2.4 %collective-permute-start.10 = (f32[128,128]{1,0:T(8,128)S(1)}, f32[128,128]{1,0:T(8,128)S(1)}, u32[]{:S(2)}, u32[]{:S(2)}) collective-permute-start(f32[128,128]{1,0:T(8,128)S(1)} %get-tuple-element.24), channel_id=1, source_target_pairs={{0,24},{4,28},{8,16},{12,20},{16,8},{20,12},{24,0},{28,4},{1,25},{... | collective-permute-start | bytes 196616 | tf_op jit(solution)/shard_map/ppermute | solution.py:102
  27.1 0.5 %collective-permute-start.11 = (f32[128,128]{1,0:T(8,128)S(1)}, f32[128,128]{1,0:T(8,128)S(1)}, u32[]{:S(2)}, u32[]{:S(2)}) collective-permute-start(f32[128,128]{1,0:T(8,128)S(1)} %get-tuple-element.25), channel_id=1, source_target_pairs={{0,16},{4,20},{8,24},{12,28},{16,0},{20,4},{24,8},{28,12},{1,17},{... | collective-permute-start | bytes 196616 | tf_op jit(solution)/shard_map/ppermute | solution.py:102
  27.6 0.7 %collective-permute-start.12 = (f32[128,128]{1,0:T(8,128)S(1)}, f32[128,128]{1,0:T(8,128)S(1)}, u32[]{:S(2)}, u32[]{:S(2)}) collective-permute-start(f32[128,128]{1,0:T(8,128)S(1)} %get-tuple-element.26), channel_id=1, source_target_pairs={{0,8},{4,12},{8,0},{12,4},{16,24},{20,28},{24,16},{28,20},{1,9},{5... | collective-permute-start | bytes 196616 | tf_op jit(solution)/shard_map/ppermute | solution.py:102
  28.3 1.7 %collective-permute-done.10 = f32[128,128]{1,0:T(8,128)S(1)} collective-permute-done((f32[128,128]{1,0:T(8,128)S(1)}, f32[128,128]{1,0:T(8,128)S(1)}, u32[]{:S(2)}, u32[]{:S(2)}) %collective-permute-start.10) | collective-permute-done | bytes 65568 | tf_op jit(solution)/shard_map/ppermute | solution.py:102
  30.0 1.4 %collective-permute-done.11 = f32[128,128]{1,0:T(8,128)S(1)} collective-permute-done((f32[128,128]{1,0:T(8,128)S(1)}, f32[128,128]{1,0:T(8,128)S(1)}, u32[]{:S(2)}, u32[]{:S(2)}) %collective-permute-start.11) | collective-permute-done | bytes 65568 | tf_op jit(solution)/shard_map/ppermute | solution.py:102
  31.4 0.5 %collective-permute-done.12 = f32[128,128]{1,0:T(8,128)S(1)} collective-permute-done((f32[128,128]{1,0:T(8,128)S(1)}, f32[128,128]{1,0:T(8,128)S(1)}, u32[]{:S(2)}, u32[]{:S(2)}) %collective-permute-start.12) | collective-permute-done | bytes 65568 | tf_op jit(solution)/shard_map/ppermute | solution.py:102
  31.9 0.6 %add_add_fusion = f32[128,128]{1,0:T(8,128)} fusion(f32[128,128]{1,0:T(8,128)S(1)} %collective-permute-done.12, f32[128,128]{1,0:T(8,128)S(1)} %collective-permute-done.11, f32[128,128]{1,0:T(8,128)S(1)} %get-tuple-element.23, f32[128,128]{1,0:T(8,128)S(1)} %collective-permute-done.10), kind=kLoop, calls=%fused_computation | loop fusion | flops 49152 | bytes 327680 | tf_op jit(solution)/shard_map/add | solution.py:179
  (6 shorter events, 0.1 us)
Async XLA Ops:
  0.0 12.4 %copy-start.1 = (f32[128,128]{1,0:T(8,128)S(1)}, f32[128,128]{1,0:T(8,128)}, u32[]{:S(2)}) copy-start(f32[128,128]{1,0:T(8,128)} %in_ref.1) | copy-start | bytes 196612
  0.0 14.6 %collective-permute-start.1 = (f32[48,512]{1,0:T(8,128)}, f32[48,512]{1,0:T(8,128)S(1)}, u32[]{:S(2)}, u32[]{:S(2)}) collective-permute-start(f32[48,512]{1,0:T(8,128)} %refs_0_.1), channel_id=1, source_target_pairs={{0,3},{1,2},{2,1},{3,0},{4,7},{5,6},{6,5},{7,4},{8,11},{9,10},{10,... | collective-permute-start | bytes 294920 | tf_op jit(solution)/shard_map/ppermute | solution.py:102
  5.1 7.4 %collective-permute-start = (f32[48,512]{1,0:T(8,128)}, f32[48,512]{1,0:T(8,128)S(1)}, u32[]{:S(2)}, u32[]{:S(2)}) collective-permute-start(f32[48,512]{1,0:T(8,128)} %refs_0_.1), channel_id=1, source_target_pairs={{0,1},{1,0},{2,3},{3,2},{4,5},{5,4},{6,7},{7,6},{8,9},{9,8},{10,11... | collective-permute-start | bytes 294920 | tf_op jit(solution)/shard_map/ppermute | solution.py:102
  5.1 9.6 %collective-permute-start.2 = (f32[48,512]{1,0:T(8,128)}, f32[48,512]{1,0:T(8,128)S(1)}, u32[]{:S(2)}, u32[]{:S(2)}) collective-permute-start(f32[48,512]{1,0:T(8,128)} %refs_0_.1), channel_id=1, source_target_pairs={{0,2},{1,3},{2,0},{3,1},{4,6},{5,7},{6,4},{7,5},{8,10},{9,11},{10,... | collective-permute-start | bytes 294920 | tf_op jit(solution)/shard_map/ppermute | solution.py:102
  5.7 12.0 %collective-permute-start.8 = (f32[128,128]{1,0:T(8,128)}, f32[128,128]{1,0:T(8,128)S(1)}, u32[]{:S(2)}, u32[]{:S(2)}) collective-permute-start(f32[128,128]{1,0:T(8,128)} %in_ref.1), channel_id=1, source_target_pairs={{0,1},{1,0},{2,3},{3,2},{4,5},{5,4},{6,7},{7,6},{8,9},{9,8},{10,11... | collective-permute-start | bytes 196616 | tf_op jit(solution)/shard_map/ppermute | solution.py:102
  7.1 0.7 %copy-start.2 = (s32[4,8]{1,0:T(4,128)S(1)}, s32[4,8]{1,0:T(4,128)}, u32[]{:S(2)}) copy-start(s32[4,8]{1,0:T(4,128)} %list_ref.1) | copy-start | bytes 388
  7.8 0.7 %copy-start.3 = (s32[4]{0:T(128)S(1)}, s32[4]{0:T(128)}, u32[]{:S(2)}) copy-start(s32[4]{0:T(128)} %count_ref.1) | copy-start | bytes 52
  12.5 7.5 %copy-start = (f32[48,512]{1,0:T(8,128)S(1)}, f32[48,512]{1,0:T(8,128)}, u32[]{:S(2)}) copy-start(f32[48,512]{1,0:T(8,128)} %refs_0_.1) | copy-start | bytes 294916
  12.5 6.2 %collective-permute-start.7 = (f32[128,128]{1,0:T(8,128)S(1)}, f32[128,128]{1,0:T(8,128)S(1)}, u32[]{:S(2)}, u32[]{:S(2)}) collective-permute-start(f32[128,128]{1,0:T(8,128)S(1)} %shard_map.48.refs_7_), channel_id=1, source_target_pairs={{0,3},{1,2},{2,1},{3,0},{4,7},{5,6},{6,5},{7,4},{8,11},{9,10},{10,... | collective-permute-start | bytes 196616 | tf_op jit(solution)/shard_map/ppermute | solution.py:102
  13.3 6.6 %collective-permute-start.6 = (f32[128,128]{1,0:T(8,128)S(1)}, f32[128,128]{1,0:T(8,128)S(1)}, u32[]{:S(2)}, u32[]{:S(2)}) collective-permute-start(f32[128,128]{1,0:T(8,128)S(1)} %shard_map.48.refs_7_), channel_id=1, source_target_pairs={{0,2},{1,3},{2,0},{3,1},{4,6},{5,7},{6,4},{7,5},{8,10},{9,11},{10,... | collective-permute-start | bytes 196616 | tf_op jit(solution)/shard_map/ppermute | solution.py:102
  14.7 6.2 %collective-permute-start.5 = (f32[200,128]{1,0:T(8,128)S(1)}, f32[200,128]{1,0:T(8,128)S(1)}, u32[]{:S(2)}, u32[]{:S(2)}) collective-permute-start(f32[200,128]{1,0:T(8,128)S(1)} %constant_dynamic-update-slice_fusion.refs_0_), channel_id=1, source_target_pairs={{0,24},{4,28},{8,16},{12,20},{16,8},{20,12},{24,0},{28,4},{1,25},{... | collective-permute-start | bytes 307208 | tf_op jit(solution)/shard_map/ppermute | solution.py:102
  17.2 4.8 %collective-permute-start.4 = (f32[200,128]{1,0:T(8,128)S(1)}, f32[200,128]{1,0:T(8,128)S(1)}, u32[]{:S(2)}, u32[]{:S(2)}) collective-permute-start(f32[200,128]{1,0:T(8,128)S(1)} %constant_dynamic-update-slice_fusion.refs_0_), channel_id=1, source_target_pairs={{0,16},{4,20},{8,24},{12,28},{16,0},{20,4},{24,8},{28,12},{1,17},{... | collective-permute-start | bytes 307208 | tf_op jit(solution)/shard_map/ppermute | solution.py:102
  17.7 4.7 %collective-permute-start.3 = (f32[200,128]{1,0:T(8,128)S(1)}, f32[200,128]{1,0:T(8,128)S(1)}, u32[]{:S(2)}, u32[]{:S(2)}) collective-permute-start(f32[200,128]{1,0:T(8,128)S(1)} %constant_dynamic-update-slice_fusion.refs_0_), channel_id=1, source_target_pairs={{0,8},{4,12},{8,0},{12,4},{16,24},{20,28},{24,16},{28,20},{1,9},{5... | collective-permute-start | bytes 307208 | tf_op jit(solution)/shard_map/ppermute | solution.py:102
  20.0 2.6 %collective-permute-start.9 = (f32[320,512]{1,0:T(8,128)S(1)}, f32[320,512]{1,0:T(8,128)S(1)}, u32[]{:S(2)}, u32[]{:S(2)}) collective-permute-start(f32[320,512]{1,0:T(8,128)S(1)} %shard_map.49.group_ref), channel_id=1, source_target_pairs={{0,4},{4,0},{8,12},{12,8},{16,20},{20,16},{24,28},{28,24},{1,5},{5... | collective-permute-start | bytes 1966088 | tf_op jit(solution)/shard_map/ppermute | solution.py:102
  24.7 5.3 %collective-permute-start.10 = (f32[128,128]{1,0:T(8,128)S(1)}, f32[128,128]{1,0:T(8,128)S(1)}, u32[]{:S(2)}, u32[]{:S(2)}) collective-permute-start(f32[128,128]{1,0:T(8,128)S(1)} %get-tuple-element.24), channel_id=1, source_target_pairs={{0,24},{4,28},{8,16},{12,20},{16,8},{20,12},{24,0},{28,4},{1,25},{... | collective-permute-start | bytes 196616 | tf_op jit(solution)/shard_map/ppermute | solution.py:102
  27.1 4.3 %collective-permute-start.11 = (f32[128,128]{1,0:T(8,128)S(1)}, f32[128,128]{1,0:T(8,128)S(1)}, u32[]{:S(2)}, u32[]{:S(2)}) collective-permute-start(f32[128,128]{1,0:T(8,128)S(1)} %get-tuple-element.25), channel_id=1, source_target_pairs={{0,16},{4,20},{8,24},{12,28},{16,0},{20,4},{24,8},{28,12},{1,17},{... | collective-permute-start | bytes 196616 | tf_op jit(solution)/shard_map/ppermute | solution.py:102
  27.6 4.3 %collective-permute-start.12 = (f32[128,128]{1,0:T(8,128)S(1)}, f32[128,128]{1,0:T(8,128)S(1)}, u32[]{:S(2)}, u32[]{:S(2)}) collective-permute-start(f32[128,128]{1,0:T(8,128)S(1)} %get-tuple-element.26), channel_id=1, source_target_pairs={{0,8},{4,12},{8,0},{12,4},{16,24},{20,28},{24,16},{28,20},{1,9},{5... | collective-permute-start | bytes 196616 | tf_op jit(solution)/shard_map/ppermute | solution.py:102
